TPU v7x, 32 devices: a whole 2x2x4 slice. The times are simulated.
32 devices in a mesh: clips: 8 (over z, x), tp: 4 (over y, core).
Axes of the slice: x: 2, y: 2, z: 4, core: 2. Of those that a mesh axis runs over, the one named last changes fastest.
Arguments:
- tokens: bfloat16 [64, 256, 768], P('clips', 'tp'), may hold values from -6 to 6
- tubelet_index: int32 [64, 256], P('clips', 'tp'), may hold values from 0 to 2559, as said below
- visible_count: int32 [64], P('clips'), may hold values from 80 to 256, as said below
- norm1_gain: float32 [768], replicated, may hold values from 0.5 to 1.5
- norm1_bias: float32 [768], replicated, may hold values from -1.5 to 1.5
- qkv_weight: bfloat16 [768, 3, 768], P(None, None, 'tp'), may hold values from -0.21875 to 0.21875
- qv_bias: float32 [2, 768], P(None, 'tp'), may hold values from -1 to 1
- proj_weight: bfloat16 [768, 768], P('tp'), may hold values from -1.75 to 1.75
- proj_bias: float32 [768], replicated, may hold values from -1.5 to 1.5
- norm2_gain: float32 [768], replicated, may hold values from 0.5 to 1.5
- norm2_bias: float32 [768], replicated, may hold values from -1.5 to 1.5
- up_weight: bfloat16 [768, 3072], P(None, 'tp'), may hold values from -0.21875 to 0.21875
- up_bias: float32 [3072], P('tp'), may hold values from -1.5 to 1.5
- down_weight: bfloat16 [3072, 768], P('tp'), may hold values from -0.109375 to 0.109375
- down_bias: float32 [768], replicated, may hold values from -1.5 to 1.5
- out_grad: bfloat16 [64, 256, 768], P('clips', 'tp'), may hold values from -6 to 6
Outputs:
- layer_out: float32 [64, 256, 768], P('clips', 'tp')
- in_grad: float32 [64, 256, 768], P('clips', 'tp')
- norm1_gain_grad: float32 [768], replicated
- norm1_bias_grad: float32 [768], replicated
- qkv_weight_grad: float32 [768, 3, 768], P(None, None, 'tp')
- qv_bias_grad: float32 [2, 768], P(None, 'tp')
- proj_weight_grad: float32 [768, 768], P('tp')
- proj_bias_grad: float32 [768], replicated
- norm2_gain_grad: float32 [768], replicated
- norm2_bias_grad: float32 [768], replicated
- up_weight_grad: float32 [768, 3072], P(None, 'tp')
- up_bias_grad: float32 [3072], P('tp')
- down_weight_grad: float32 [3072, 768], P('tp')
- down_bias_grad: float32 [768], replicated
Inputs may be any that keep to these rules, and one draw needn't show every extreme that they name: `visible_count`: each clip has 80, 160 or 256 visible tubelets, in its first slots; some clip has 256. `tubelet_index`: slot j of a clip holds an index from 10 * j to 10 * j + 9.
All inputs are finite; a program needn't handle non-finite values.
Results may differ from a plain program's by a relative error of at most 0.019.
Values may be sent and summed in bfloat16 or wider, within the bound.
A program may use at most 128 MiB of HBM per device.

v0:
```python
import functools
import math

import jax
import jax.numpy as jnp
import numpy as np
from jax import lax
from jax.experimental import pallas as pl
from jax.experimental.pallas import tpu as pltpu
from jax.sharding import PartitionSpec as P

HD = 64
EPSILON = 1e-06
NEGATIVE = -1000000000.0
BF = jnp.bfloat16
F32 = jnp.float32
MESH = pl.DeviceIdType.MESH
VMEM_LIMIT = 62 * 2**20
CHUNK = 128
F_BLOCK = 256
ROWS = 128
N_TP = 4
TABLE = 64
NN = (((1,), (0,)), ((), ()))
NT = (((1,), (1,)), ((), ()))
TN = (((0,), (0,)), ((), ()))


def dot(a, b, dims):
    return lax.dot_general(a, b, dims, preferred_element_type=F32)


def flip(value, weight):
    return value + weight - 2 * weight * lax.rem(lax.div(value, weight), 2)


def bit_of(value, weight):
    return lax.rem(lax.div(value, weight), 2)


def aligned(value, multiple=16):
    return value if isinstance(value, int) else pl.multiple_of(value, multiple)


def gelu_parts(x):
    e = jnp.exp(-0.5 * x * x)
    z = jnp.abs(x) * (0.3275911 / math.sqrt(2.0))
    r = 1.0 / (1.0 + z)
    poly = r * (0.254829592 + r * (-0.284496736 + r * (1.421413741 + r * (-1.453152027 + r * 1.061405429))))
    tail = 0.5 * poly * e
    cdf = jnp.where(x >= 0, 1.0 - tail, tail)
    return x * cdf, cdf + x * (e * (1.0 / math.sqrt(2.0 * math.pi)))


def stats(v):
    mean = jnp.mean(v, axis=-1, keepdims=True)
    center = v - mean
    rstd = lax.rsqrt(jnp.mean(center * center, axis=-1, keepdims=True) + EPSILON)
    return center * rstd, rstd


def norm_back(v, dy, gain):
    xhat, rstd = stats(v)
    dx = dy * gain
    m1 = jnp.mean(dx, axis=-1, keepdims=True)
    m2 = jnp.mean(dx * xhat, axis=-1, keepdims=True)
    return (dx - m1 - xhat * m2) * rstd, jnp.sum(dy * xhat, axis=0, keepdims=True), jnp.sum(dy, axis=0, keepdims=True)


def reduce_stages(n_clips):
    stages = []
    rows = CHUNK
    weight = 1
    while weight < n_clips:
        halving = rows >= 32
        if halving:
            rows //= 2
        stages.append((weight, rows, halving))
        weight *= 2
    return stages


def layer_kernel(dims, stages, lags, count_ref, tok_ref, ext_ref, og_ref, proj_ref, qkv_ref, up_ref, down_ref, vec_ref,
                 bias_ref, table_ref, grad_ref, small_ref, res_ref, ing_ref,
                 w, tokb, extb, ogb, biasb, stream, first, qkvt, probs, mixed, middle, second, ff, sg, branch, outp, inp,
                 core_buf, side_buf, *rest):
    here, slots, width, hidden, features = dims
    bufs = rest[: len(stages)]
    small_buf, l_sem, t_sem, y_sem, q_sem, f_sem, c_sem, r_sem, s_sem, o_sem = rest[len(stages):]
    c = lax.axis_index("clips")
    t = lax.axis_index("tp")
    k, u = bit_of(t, 1), bit_of(t, 2)
    core = (c, flip(t, 1))
    side = (c, flip(t, 2))
    across = (flip(c, 1), t)
    along = (flip(c, 2), t)
    others = [(c, lax.rem(t + i, N_TP)) for i in range(1, N_TP)]
    peers = [(flip(c, weight), t) for weight, _, _ in stages]
    own_slots = slots // N_TP
    n_rows = here * slots
    a_rows = 4 * width
    total_rows = a_rows + 2 * hidden
    nf = hidden // F_BLOCK
    blocks = [(0, a_rows)] + [(a_rows + 2 * F_BLOCK * j, 2 * F_BLOCK) for j in range(nf)]
    n_chunks = total_rows // CHUNK
    b0, b1 = bit_of(c, 1), bit_of(c, 2)
    quarter = b1 * 2 + b0
    via_z = (1 - b1) * 2 + b0
    via_x = b1 * 2 + (1 - b0)

    pieces = [[(proj_ref, 0, 0, width), (qkv_ref, 0, width, 3 * width)]]
    for j in range(nf):
        base = a_rows + 2 * F_BLOCK * j
        pieces.append([(up_ref, j * F_BLOCK, base, F_BLOCK), (down_ref, j * F_BLOCK, base + F_BLOCK, F_BLOCK)])

    def own_copies(i):
        return [pltpu.make_async_copy(ref.at[pl.ds(at, rows)], w.at[u, k, pl.ds(to, rows)], l_sem.at[i, n])
                for n, (ref, at, to, rows) in enumerate(pieces[i])]

    def row_copies():
        return [pltpu.make_async_copy(src.at[pl.ds(t * here, here)], dst.at[:, pl.ds(t * own_slots, own_slots)],
                                      l_sem.at[nf + 1, n])
                for n, (src, dst) in enumerate(((tok_ref, tokb), (ext_ref, extb), (og_ref, ogb)))] + [
                    pltpu.make_async_copy(bias_ref, biasb.at[t], l_sem.at[nf + 1, 3])]

    for i in range(nf + 1):
        for copy in own_copies(i):
            copy.start()
    for copy in row_copies():
        copy.start()

    barrier = pltpu.get_barrier_semaphore()
    targets = others + peers
    for target in targets:
        pl.semaphore_signal(barrier, inc=1, device_id=target, device_id_type=MESH)
    pl.semaphore_wait(barrier, len(targets))

    def remote(src, dst, sem, index, target):
        return pltpu.make_async_remote_copy(src_ref=src, dst_ref=dst, send_sem=sem.at[(0, *index)],
                                            recv_sem=sem.at[(1, *index)], device_id=target, device_id_type=MESH)

    def rows_copy(n, i):
        target = others[i]
        if n == 3:
            return remote(bias_ref, biasb.at[t], t_sem, (n, i), target)
        src = (tok_ref, ext_ref, og_ref)[n]
        dst = (tokb, extb, ogb)[n]
        return remote(src.at[pl.ds(target[1] * here, here)], dst.at[:, pl.ds(t * own_slots, own_slots)], t_sem,
                      (n, i), target)

    def w_copy(kind, i):
        base, rows = blocks[i]
        q, h = rows // 4, rows // 8
        su, start, size, sem, index, target = {
            "y": (u, base + quarter * q, q, y_sem, (i,), side),
            "x": (1 - u, base + quarter * q, q, q_sem, (0, i), across),
            "z": (1 - u, base + quarter * q, q, q_sem, (1, i), along),
            "xf": (1 - u, base + via_z * q, h, f_sem, (0, i), across),
            "zf": (1 - u, base + via_x * q + h, h, f_sem, (1, i), along),
            "co": (u, base, rows, c_sem, (0, i), core),
            "cf": (1 - u, base, rows, c_sem, (1, i), core),
        }[kind]
        view = w.at[su, k, pl.ds(aligned(start), size)]
        return remote(view, view, sem, index, target)

    def begin(i):
        for copy in own_copies(i):
            copy.wait()
        w_copy("y", i).start()
        w_copy("co", i).start()

    def step1(i):
        w_copy("y", i).wait_recv()
        w_copy("x", i).start()
        w_copy("z", i).start()

    def step2(i):
        w_copy("z", i).wait_recv()
        w_copy("xf", i).start()
        w_copy("x", i).wait_recv()
        w_copy("zf", i).start()

    def step3(i):
        w_copy("xf", i).wait_recv()
        w_copy("zf", i).wait_recv()
        w_copy("cf", i).start()

    def step4(i):
        w_copy("co", i).wait_recv()
        w_copy("cf", i).wait_recv()
        for kind in ("y", "x", "z", "xf", "zf", "co", "cf"):
            w_copy(kind, i).wait_send()

    def start_rows(n):
        for i in range(N_TP - 1):
            rows_copy(n, i).start()

    def wait_rows(n):
        for i in range(N_TP - 1):
            rows_copy(n, i).wait_recv()

    begin(0)
    start_rows(3)
    start_rows(1)
    start_rows(0)
    for i in range(1, nf + 1):
        begin(i)
        if i == 1:
            start_rows(2)

    small_ref[...] = jnp.zeros_like(small_ref)
    ff[...] = jnp.zeros_like(ff)
    sg[...] = jnp.zeros_like(sg)

    step1(0)
    for copy in row_copies():
        copy.wait()
    wait_rows(3)
    wait_rows(1)
    wait_rows(0)
    half = features // 2

    def vec(i):
        return vec_ref[pl.ds(i, 1), :]

    def first_rows(i, _):
        b, at = lax.div(i, slots // ROWS), lax.rem(i, slots // ROWS) * ROWS
        rows = pl.ds(pl.multiple_of(i * ROWS, ROWS), ROWS)
        here_rows = pl.ds(pl.multiple_of(at, ROWS), ROWS)
        place = extb[b, here_rows, :].astype(F32)
        lane = lax.broadcasted_iota(jnp.int32, (ROWS, 2 * TABLE), 1)
        lane = lax.rem(lane, TABLE).astype(F32)
        hot_hi = jnp.where(lane == place[:, 0:1], 1.0, 0.0).astype(BF)
        hot_lo = jnp.where(lane == place[:, 1:2], 1.0, 0.0).astype(BF)
        hi = dot(hot_hi, table_ref[0 : 2 * TABLE, :], NN)
        lo = dot(hot_lo, table_ref[2 * TABLE :, :], NN)
        sh, ch, sl, cl = hi[:, :half], hi[:, half:], lo[:, :half], lo[:, half:]
        pos = jnp.concatenate([sh * cl + ch * sl, ch * cl - sh * sl], axis=1)
        v = tokb[b, here_rows, :].astype(F32) + pos
        stream[rows, :] = v
        xhat, _ = stats(v)
        first[rows, :] = (xhat * vec(0) + vec(1)).astype(BF)
        return 0

    lax.fori_loop(0, n_rows // ROWS, first_rows, 0)
    step2(0)
    step1(1)
    step3(0)
    step4(0)

    scale = HD ** -0.5

    def qkv_of(g, _):
        gu, gk = lax.div(g, 2), lax.rem(g, 2)
        out = dot(w[gu, gk, width:a_rows, :], first[...], NT)
        out = out + biasb[g, :, 0:BIAS_UP].T[0 : 3 * width, 0:1]
        qkvt[g, 0:width, :] = (out[0:width].astype(BF).astype(F32) * scale).astype(BF)
        qkvt[g, width : 3 * width, :] = out[width : 3 * width].astype(BF)
        return 0

    lax.fori_loop(0, N_TP, qkv_of, 0)
    step2(1)
    step1(2)

    per_group = width // HD

    def attend(g, _):
        for b in range(here):
            cols = slice(b * slots, (b + 1) * slots)
            visible = count_ref[t * here + b]
            keep = lax.broadcasted_iota(jnp.int32, (slots, slots), 0) < visible
            for r in range(per_group):
                q = qkvt[g, r * HD : (r + 1) * HD, cols]
                key = qkvt[g, width + r * HD : width + (r + 1) * HD, cols]
                value = qkvt[g, 2 * width + r * HD : 2 * width + (r + 1) * HD, cols]
                s = jnp.where(keep, dot(key, q, TN), NEGATIVE)
                e = jnp.exp(s - jnp.max(s, axis=0, keepdims=True))
                p = (e * (1.0 / jnp.sum(e, axis=0, keepdims=True))).astype(BF)
                probs[b, g * per_group + r] = p
                mixed[g, r * HD : (r + 1) * HD, cols] = dot(value, p, NN).astype(BF)

        @pl.when(g == 0)
        def _():
            step3(1)

        @pl.when(g == 1)
        def _():
            step2(2)

        @pl.when(g == 2)
        def _():
            step1(3)

        return 0

    lax.fori_loop(0, N_TP, attend, 0)

    def second_rows(i, _):
        rows = pl.ds(pl.multiple_of(i * ROWS, ROWS), ROWS)
        total = stream[rows, :] + vec(4)
        for g in range(N_TP):
            total = total + dot(mixed[g, :, rows], w[g // 2, g % 2, 0:width, :], TN)
        middle[rows, :] = total
        xhat, _ = stats(total)
        second[rows, :] = (xhat * vec(2) + vec(3)).astype(BF)
        return 0

    lax.fori_loop(0, n_rows // ROWS, second_rows, 0)
    wait_rows(2)

    def kept(stage, chunk):
        start = chunk * CHUNK
        for weight, rows, halving in stages[:stage]:
            if halving:
                start = start + bit_of(c, weight) * rows
        return start

    n_rs = 2 + len(stages)
    halvings = [i for i, s in enumerate(stages) if s[2]]
    gathers = list(reversed(halvings))
    n_all = n_rs + len(gathers)

    def shifted(chunk):
        return lax.rem(chunk + a_rows // CHUNK, n_chunks)

    def copy_of(stage, chunk):
        at = shifted(chunk)
        rows = pl.ds(aligned(at * CHUNK), CHUNK)
        if stage == 0:
            src, dst, target = w.at[:, 1 - k, rows], core_buf.at[:, rows], core
        elif stage == 1:
            src, dst, target = core_buf.at[1 - u, rows], side_buf.at[rows], side
        elif stage < n_rs:
            i = stage - 2
            weight, size, halving = stages[i]
            start = kept(i, at)
            if halving:
                start = start + (1 - bit_of(c, weight)) * size
            src = side_buf.at[pl.ds(aligned(start), size)]
            dst = bufs[i].at[pl.ds(aligned(at * size), size)]
            target = peers[i]
        else:
            i = gathers[stage - n_rs]
            size = stages[i][1]
            src = grad_ref.at[pl.ds(aligned(kept(i + 1, at)), size)]
            dst, target = src, peers[i]
        return remote(src, dst, r_sem, (stage, chunk), target)

    def add(a, b):
        return (a.astype(F32) + b.astype(F32)).astype(BF)

    def finish(stage, chunk):
        copy_of(stage, chunk).wait_recv()
        at = shifted(chunk)
        rows = pl.ds(aligned(at * CHUNK), CHUNK)
        if stage == 0:
            for n in (0, 1):
                core_buf[n, rows] = add(w[n, k, rows], core_buf[n, rows])
        elif stage == 1:
            side_buf[rows] = add(core_buf[u, rows], side_buf[rows])
        elif stage < n_rs:
            i = stage - 2
            _, size, halving = stages[i]
            keep_rows = pl.ds(aligned(kept(i + 1, at)), size)
            if not halving:
                copy_of(stage, chunk).wait_send()
            result = grad_ref if stage == n_rs - 1 else side_buf
            result[keep_rows] = add(side_buf[keep_rows], bufs[i][pl.ds(aligned(at * size), size)])

    starts = [0]
    for lag in lags[:n_all]:
        starts.append(starts[-1] + lag)

    def tick(i):
        for stage in reversed(range(n_all + 1)):
            chunk = i - starts[stage]

            @pl.when((chunk >= 0) & (chunk < n_chunks))
            def _():
                if stage > 0:
                    finish(stage - 1, chunk)
                if stage < n_all:
                    copy_of(stage, chunk).start()

    per_block = 2 * F_BLOCK // CHUNK

    def ffn(i, _):
        j, g = lax.div(i, N_TP), lax.rem(i, N_TP)
        gu, gk = lax.div(g, 2), lax.rem(g, 2)

        @pl.when(i == 0)
        def _():
            step4(1)
            step2(3)
            step3(2)

        @pl.when(i == N_TP)
        def _():
            step4(2)
            step3(3)

        @pl.when(i == 2 * N_TP)
        def _():
            step4(3)

        base = a_rows + j * 2 * F_BLOCK
        up_rows = pl.ds(pl.multiple_of(base, F_BLOCK), F_BLOCK)
        down_rows = pl.ds(pl.multiple_of(base + F_BLOCK, F_BLOCK), F_BLOCK)
        up, down = w[gu, gk, up_rows, :], w[gu, gk, down_rows, :]
        lanes = pl.ds(pl.multiple_of(BIAS_UP + j * F_BLOCK, F_BLOCK // 2), F_BLOCK)
        pre = dot(second[...], up, NT) + biasb[g, 0:1, lanes]
        act, slope = gelu_parts(pre)
        act = act.astype(BF)
        ff[...] += dot(act, down, NN)
        og = ogb[...].reshape(n_rows, features)
        pg = (dot(og, down, NT) * slope).astype(BF)
        sg[...] += dot(pg, up, NN)
        w[gu, gk, down_rows, :] = dot(act, og, TN).astype(BF)
        w[gu, gk, up_rows, :] = dot(pg, second[...], TN).astype(BF)
        small_ref[pl.ds(8 + g, 1), pl.ds(pl.multiple_of(j * F_BLOCK, F_BLOCK), F_BLOCK)] = jnp.sum(
            pg.astype(F32), axis=0, keepdims=True)

        @pl.when(i >= N_TP)
        def _():
            tick(i - N_TP)

        return 0

    lax.fori_loop(0, nf * N_TP, ffn, 0)
    done = (nf - 1) * N_TP

    def middle_rows(i, _):
        b, at = lax.div(i, slots // ROWS), lax.rem(i, slots // ROWS) * ROWS
        rows = pl.ds(pl.multiple_of(i * ROWS, ROWS), ROWS)
        here_rows = pl.ds(pl.multiple_of(at, ROWS), ROWS)
        m = middle[rows, :]
        outp[b, here_rows, :] = (m + ff[rows, :] + vec(5)).astype(BF)
        dv, dgain, dbias = norm_back(m, sg[rows, :], vec(2))
        og = ogb[b, here_rows, :].astype(F32)
        mg = og + dv
        ff[rows, :] = mg
        bg = mg.astype(BF)
        branch[rows, :] = bg
        small_ref[2:3, :] += dgain
        small_ref[3:4, :] += dbias
        small_ref[4:5, :] += jnp.sum(bg.astype(F32), axis=0, keepdims=True)
        small_ref[5:6, :] += jnp.sum(og, axis=0, keepdims=True)
        return 0

    lax.fori_loop(0, n_rows // ROWS, middle_rows, 0)

    def back_copy(n, i):
        src, dst = ((outp, res_ref), (inp, ing_ref))[n]
        target = others[i]
        return remote(src.at[:, pl.ds(target[1] * own_slots, own_slots)], dst.at[pl.ds(t * here, here)], o_sem,
                      (n, i), target)

    def back_own(n):
        src, dst = ((outp, res_ref), (inp, ing_ref))[n]
        return pltpu.make_async_copy(src.at[:, pl.ds(t * own_slots, own_slots)], dst.at[pl.ds(t * here, here)],
                                     l_sem.at[nf + 2, n])

    def send_back(n):
        back_own(n).start()
        for i in range(N_TP - 1):
            back_copy(n, i).start()

    send_back(0)
    sg[...] = jnp.zeros_like(sg)

    def back_group(g, _):
        gu, gk = lax.div(g, 2), lax.rem(g, 2)
        bg = branch[...]
        pw = w[gu, gk, 0:width, :]
        dmix = dot(pw, bg, NT).astype(BF)
        w[gu, gk, 0:width, :] = dot(mixed[g], bg, NN).astype(BF)
        for b in range(here):
            cols = slice(b * slots, (b + 1) * slots)
            for r in range(per_group):
                q_rows = slice(r * HD, (r + 1) * HD)
                k_rows = slice(width + r * HD, width + (r + 1) * HD)
                v_rows = slice(2 * width + r * HD, 2 * width + (r + 1) * HD)
                q, key, value = qkvt[g, q_rows, cols], qkvt[g, k_rows, cols], qkvt[g, v_rows, cols]
                dm = dmix[q_rows, cols]
                p = probs[b, g * per_group + r]
                pf = p.astype(F32)
                dp = dot(value, dm, TN)
                ds = (pf * (dp - jnp.sum(pf * dp, axis=0, keepdims=True))).astype(BF)
                qkvt[g, q_rows, cols] = (dot(key, ds, NN) * scale).astype(BF)
                qkvt[g, k_rows, cols] = dot(q, ds, NT).astype(BF)
                qkvt[g, v_rows, cols] = dot(dm, p, NT).astype(BF)
        dqkv = qkvt[g]
        sg[...] += dot(dqkv, w[gu, gk, width:a_rows, :], TN)
        w[gu, gk, width:a_rows, :] = dot(dqkv, first[...], NN).astype(BF)
        small_ref[pl.ds(12 + g, 1), 0 : 3 * width] = dot(jnp.ones((8, n_rows), BF), dqkv, NT)[0:1]
        tick(done + g)
        return 0

    lax.fori_loop(0, N_TP, back_group, 0)

    def last_rows(i, _):
        b, at = lax.div(i, slots // ROWS), lax.rem(i, slots // ROWS) * ROWS
        rows = pl.ds(pl.multiple_of(i * ROWS, ROWS), ROWS)
        here_rows = pl.ds(pl.multiple_of(at, ROWS), ROWS)
        dv, dgain, dbias = norm_back(stream[rows, :], sg[rows, :], vec(0))
        inp[b, here_rows, :] = (ff[rows, :] + dv).astype(BF)
        small_ref[0:1, :] += dgain
        small_ref[1:2, :] += dbias
        return 0

    lax.fori_loop(0, n_rows // ROWS, last_rows, 0)
    send_back(1)

    small_targets = [core, side] + peers

    def small_copy(i):
        return remote(small_ref, small_buf.at[i], s_sem, (i,), small_targets[i])

    done = done + N_TP

    def rest_of(i, _):
        for n in range(len(small_targets) + 1):
            @pl.when(i == done + n)
            def _():
                if n > 0:
                    small_copy(n - 1).wait()
                    small_ref[...] += small_buf[n - 1]
                if n < len(small_targets):
                    small_copy(n).start()
        tick(i)
        return 0

    lax.fori_loop(done, n_chunks + starts[-1], rest_of, 0)

    for n in (0, 1):
        for i in range(N_TP - 1):
            back_copy(n, i).wait_recv()
            back_copy(n, i).wait_send()
        back_own(n).wait()
    for n in range(4):
        for i in range(N_TP - 1):
            rows_copy(n, i).wait_send()

    def drain(chunk, _):
        for stage in range(n_all):
            if 2 <= stage < n_rs and not stages[stage - 2][2]:
                continue
            copy_of(stage, chunk).wait_send()
        return 0

    lax.fori_loop(0, n_chunks, drain, 0)


BIAS_UP = 640


def layer_call(n_clips, counts, tok, ext, og, proj, qkv, up, down, vectors, biases, table):
    count, own_slots, features = tok.shape
    width = proj.shape[0]
    hidden = up.shape[0]
    here = count // N_TP
    slots = own_slots * N_TP
    n_rows = here * slots
    rows = 4 * width + 2 * hidden
    nf = hidden // F_BLOCK
    n_chunks = rows // CHUNK
    heads = features // HD
    stages = reduce_stages(n_clips)
    n_all = 2 + len(stages) + sum(1 for s in stages if s[2])
    lags = [1, 2, 2] + [1] * (n_all - 4) + [2]
    hbm = pl.BlockSpec(memory_space=pl.ANY)
    vmem = pl.BlockSpec(memory_space=pltpu.VMEM)
    smem = pl.BlockSpec(memory_space=pltpu.SMEM)
    dma = pltpu.SemaphoreType.DMA
    nb = nf + 1
    return pl.pallas_call(
        functools.partial(layer_kernel, (here, slots, width, hidden, features), stages, lags),
        out_shape=(
            jax.ShapeDtypeStruct((rows, features), BF),
            jax.ShapeDtypeStruct((16, features), F32),
            jax.ShapeDtypeStruct((count, own_slots, features), BF),
            jax.ShapeDtypeStruct((count, own_slots, features), BF),
        ),
        in_specs=[smem, hbm, hbm, hbm, hbm, hbm, hbm, hbm, vmem, vmem, vmem],
        out_specs=(vmem, vmem, hbm, hbm),
        scratch_shapes=[
            pltpu.VMEM((2, 2, rows, features), BF),
            pltpu.VMEM((here, slots, features), BF),
            pltpu.VMEM((here, slots, 128), BF),
            pltpu.VMEM((here, slots, features), BF),
            pltpu.VMEM((N_TP, *biases.shape), F32),
            pltpu.VMEM((n_rows, features), F32),
            pltpu.VMEM((n_rows, features), BF),
            pltpu.VMEM((N_TP, 3 * width, n_rows), BF),
            pltpu.VMEM((here, heads, slots, slots), BF),
            pltpu.VMEM((N_TP, width, n_rows), BF),
            pltpu.VMEM((n_rows, features), F32),
            pltpu.VMEM((n_rows, features), BF),
            pltpu.VMEM((n_rows, features), F32),
            pltpu.VMEM((n_rows, features), F32),
            pltpu.VMEM((n_rows, features), BF),
            pltpu.VMEM((here, slots, features), BF),
            pltpu.VMEM((here, slots, features), BF),
            pltpu.VMEM((2, rows, features), BF),
            pltpu.VMEM((rows, features), BF),
            *[pltpu.VMEM((n_chunks * size, features), BF) for _, size, _ in stages],
            pltpu.VMEM((2 + len(stages), 16, features), F32),
            dma((nf + 3, 4)),
            dma((2, 4, N_TP - 1)),
            dma((2, nb)),
            dma((2, 2, nb)),
            dma((2, 2, nb)),
            dma((2, 2, nb)),
            dma((2, n_all, n_chunks)),
            dma((2, 2 + len(stages))),
            dma((2, 2, N_TP - 1)),
        ],
        compiler_params=pltpu.CompilerParams(collective_id=0, has_side_effects=True, vmem_limit_bytes=VMEM_LIMIT),
        name="encoder_layer",
    )(counts, tok, ext, og, proj, qkv, up, down, vectors, biases, table)


def place_table(features, largest):
    half = features // 2
    freq = np.exp(-math.log(10000.0) * np.arange(half, dtype=np.float64) / half).astype(np.float32).astype(np.float64)
    parts = []
    for step in (TABLE, 1):
        angle = step * np.arange(TABLE, dtype=np.float64)[:, None] * freq
        values = np.concatenate([np.sin(angle), np.cos(angle)], axis=1).astype(np.float32)
        high = values.astype(BF)
        parts += [high, (values - high.astype(np.float32)).astype(BF)]
    return np.concatenate(parts, axis=0)


def per_device(n_clips, tokens, tubelet_index, visible_count, norm1_gain, norm1_bias, qkv_weight, qv_bias,
               proj_weight, proj_bias, norm2_gain, norm2_bias, up_weight, up_bias, down_weight, down_bias, out_grad):
    count, rows, features = tokens.shape
    width = qkv_weight.shape[2]
    hidden = up_weight.shape[1]
    t = lax.axis_index("tp")
    qkv_t = jnp.transpose(qkv_weight, (1, 2, 0)).reshape(3 * width, features)
    up_t = up_weight.T
    hi = (tubelet_index // TABLE).astype(BF)[..., None]
    lo = (tubelet_index % TABLE).astype(BF)[..., None]
    lane = jnp.arange(128)[None, None, :]
    ext = jnp.where(lane == 0, hi, jnp.where(lane == 1, lo, jnp.zeros((), BF)))
    zeros = jnp.zeros((width,), F32)
    line = jnp.concatenate([qv_bias[0], zeros, qv_bias[1], jnp.zeros((BIAS_UP - 3 * width,), F32), up_bias])
    biases = jnp.zeros((8, line.shape[0]), F32).at[0].set(line)
    none = jnp.zeros((features,), F32)
    vectors = jnp.stack([norm1_gain, norm1_bias, norm2_gain, norm2_bias, proj_bias, down_bias, none, none])
    table = jnp.asarray(place_table(features, 2560))
    total, small, rows_out, rows_in = layer_call(
        n_clips, visible_count, tokens, ext, out_grad, proj_weight, qkv_t, up_t, down_weight, vectors, biases, table)
    total = total.astype(F32)
    a_rows = 4 * width
    nf = hidden // F_BLOCK
    ffn_grad = total[a_rows:].reshape(nf, 2, F_BLOCK, features)
    qkv_out = jnp.transpose(total[width:a_rows].reshape(3, width, features), (2, 0, 1))
    qkv_b = lax.dynamic_slice(small, (12 + t, 0), (1, features))[0]
    qv_out = jnp.stack([qkv_b[:width], qkv_b[2 * width : 3 * width]])
    up_b = lax.dynamic_slice(small, (8 + t, 0), (1, features))[0]
    return (
        rows_out.astype(F32),
        rows_in.astype(F32),
        small[0],
        small[1],
        qkv_out,
        qv_out,
        total[:width],
        small[4],
        small[2],
        small[3],
        ffn_grad[:, 0].reshape(hidden, features).T,
        up_b,
        ffn_grad[:, 1].reshape(hidden, features),
        small[5],
    )


def solution(mesh):
    placed = (
        P("clips", "tp", None), P("clips", "tp"), P("clips"), P(), P(), P(None, None, "tp"), P(None, "tp"),
        P("tp", None), P(), P(), P(), P(None, "tp"), P("tp"), P("tp", None), P(), P("clips", "tp", None),
    )
    return jax.shard_map(
        functools.partial(per_device, mesh.shape["clips"]),
        mesh=mesh,
        in_specs=placed,
        out_specs=(
            P("clips", "tp", None), P("clips", "tp", None), P(), P(), P(None, None, "tp"), P(None, "tp"),
            P("tp", None), P(), P(), P(), P(None, "tp"), P("tp"), P("tp", None), P(),
        ),
        check_vma=False,
    )
```

profile of v0, /device:TPU:0, one launch (start us, length us, event | category | flops | bytes accessed | tf_op | source)
XLA Modules:
  0.0 224.6 jit_solution(2286786583064927538)
XLA Ops:
  0.6 0.0 copy-start.3
  0.7 0.0 copy-start.4
  0.7 0.0 copy-start.5
  0.7 0.0 copy-start.6
  0.7 0.0 copy-start.7
  0.7 0.0 copy-start.8
  0.7 0.7 fusion
  1.4 0.9 select_select_fusion.ext_ref
  2.3 0.8 fusion.5
  3.1 0.8 concatenate.5
  3.8 0.6 scatter.4.bias_ref
  4.5 2.4 %copy.33 = bf16[768,768]{0,1:T(8,128)(2,1)} copy(bf16[768,768]{1,0:T(8,128)(2,1)} %param.30) | data formatting | bytes 2359296 | tf_op args[11]
  6.8 0.0 copy-done.3
  6.8 0.0 copy-done.4
  6.9 0.0 copy-done.5
  6.9 0.0 copy-done.6
  6.9 0.0 copy-done.7
  6.9 0.0 copy-done.8
  7.0 0.6 stack.36.vec_ref
  7.6 201.2 %encoder_layer.1 = (bf16[2304,768]{1,0:T(8,128)(2,1)}, f32[16,768]{1,0:T(8,128)}, bf16[8,64,768]{2,1,0:T(8,128)(2,1)}, bf16[8,64,768]{2,1,0:T(8,128)(2,1)}) custom-call(s32[8]{0:T(128)} %count_ref.1, bf16[8,64,768]{2,1,0:T(8,128)(2,1)} %tok_ref.1, bf16[8,64,128]{2,1,0:T(8,128)(2,1)} %select_select_fusion.ext_ref, bf16[8,64,768]{2,1,0:T(8,128)(2,1)} %og_ref.1, ...), custom_call_target="tpu_custom_call" | custom-call | tf_op jit(solution)/shard_map/encoder_layer/pallas_call | solution.py:576
  208.8 0.8 constant_dynamic-slice_fusion
  209.6 0.6 pad_maximum_fusion
  210.2 1.6 slice_reduce_fusion
  211.9 2.0 slice.78
  213.9 2.8 %fusion.4 = (f32[3,1,256,768]{3,2,1,0:T(8,128)}, f32[3,1,256,768]{3,2,1,0:T(8,128)}) fusion(f32[3,2,256,768]{3,2,1,0:T(8,128)S(1)} %bitcast.16), kind=kLoop, calls=%fused_computation.22 | loop fusion | bytes 9437184 | tf_op jit(solution)/shard_map/slice | solution.py:676
  216.7 3.2 %copy.35 = f32[768,768]{1,0:T(8,128)} copy(f32[768,768]{0,1:T(8,128)} %bitcast.17) | data formatting | bytes 4718592
  219.8 0.0 copy-done
  219.9 1.3 slice.76
  221.2 0.9 slice.77
  222.0 0.0 copy-done.2
  222.0 1.3 convert_element_type.17
  223.3 1.3 convert_element_type.18
  (15 shorter events, 0.1 us)
Async XLA Ops:
  0.6 6.2 %copy-start.3 = (f32[768]{0:T(1024)S(1)}, f32[768]{0:T(1024)}, u32[]{:S(2)}) copy-start(f32[768]{0:T(1024)} %param.22) | copy-start | bytes 9220
  0.7 6.2 %copy-start.4 = (f32[768]{0:T(1024)S(1)}, f32[768]{0:T(1024)}, u32[]{:S(2)}) copy-start(f32[768]{0:T(1024)} %param.23) | copy-start | bytes 9220
  0.7 6.2 %copy-start.5 = (f32[768]{0:T(1024)S(1)}, f32[768]{0:T(1024)}, u32[]{:S(2)}) copy-start(f32[768]{0:T(1024)} %param.28) | copy-start | bytes 9220
  0.7 6.2 %copy-start.6 = (f32[768]{0:T(1024)S(1)}, f32[768]{0:T(1024)}, u32[]{:S(2)}) copy-start(f32[768]{0:T(1024)} %param.29) | copy-start | bytes 9220
  0.7 6.2 %copy-start.7 = (f32[768]{0:T(1024)S(1)}, f32[768]{0:T(1024)}, u32[]{:S(2)}) copy-start(f32[768]{0:T(1024)} %param.27) | copy-start | bytes 9220
  0.7 6.2 %copy-start.8 = (f32[768]{0:T(1024)S(1)}, f32[768]{0:T(1024)}, u32[]{:S(2)}) copy-start(f32[768]{0:T(1024)} %param.33) | copy-start | bytes 9220
  216.7 3.2 %copy-start = (bf16[2304,768]{1,0:T(8,128)(2,1)S(1)}, bf16[2304,768]{1,0:T(8,128)(2,1)}, u32[]{:S(2)}) copy-start(bf16[2304,768]{1,0:T(8,128)(2,1)} %get-tuple-element.33) | copy-start | bytes 10616836
  219.8 2.2 copy-start.2
  221.2 2.1 copy-start.1
where the time goes:
time: 225 us
  Pallas kernels  201 us (89%)
  local copies, waits for them, and re-layouts  17.8 us (8%)
  other arithmetic  4.74 us (2%)
    pallas_call x1, Pallas kernels, layer_call(): pl.pallas_call(functools.partial(layer_kernel, (here, slots, width, hidde...  201 us
    unnamed x20, local copies, waits for them, and re-layouts  5.6 us

commit v1 on v0

v1 whole, which is shorter than its diff:
```python
import functools
import math

import jax
import jax.numpy as jnp
import numpy as np
from jax import lax
from jax.experimental import pallas as pl
from jax.experimental.pallas import tpu as pltpu
from jax.sharding import PartitionSpec as P

HD = 64
EPSILON = 1e-06
NEGATIVE = -1000000000.0
BF = jnp.bfloat16
F32 = jnp.float32
MESH = pl.DeviceIdType.MESH
VMEM_LIMIT = 62 * 2**20
CHUNK = 128
F_BLOCK = 256
ROWS = 128
N_TP = 4
TABLE = 64
NN = (((1,), (0,)), ((), ()))
NT = (((1,), (1,)), ((), ()))
TN = (((0,), (0,)), ((), ()))


def dot(a, b, dims):
    return lax.dot_general(a, b, dims, preferred_element_type=F32)


def flip(value, weight):
    return value + weight - 2 * weight * lax.rem(lax.div(value, weight), 2)


def bit_of(value, weight):
    return lax.rem(lax.div(value, weight), 2)


def row(ref):
    return ref[...].reshape(1, ref.shape[0])


def div(value, by):
    return value // by if isinstance(value, int) else lax.div(value, by)


def mod(value, by):
    return value % by if isinstance(value, int) else lax.rem(value, by)


def aligned(value, multiple=16):
    return value if isinstance(value, int) else pl.multiple_of(value, multiple)


def gelu_parts(x):
    e = jnp.exp(-0.5 * x * x)
    z = jnp.abs(x) * (0.3275911 / math.sqrt(2.0))
    r = 1.0 / (1.0 + z)
    poly = r * (0.254829592 + r * (-0.284496736 + r * (1.421413741 + r * (-1.453152027 + r * 1.061405429))))
    tail = 0.5 * poly * e
    cdf = jnp.where(x >= 0, 1.0 - tail, tail)
    return x * cdf, cdf + x * (e * (1.0 / math.sqrt(2.0 * math.pi)))


def stats(v):
    mean = jnp.mean(v, axis=-1, keepdims=True)
    center = v - mean
    rstd = lax.rsqrt(jnp.mean(center * center, axis=-1, keepdims=True) + EPSILON)
    return center * rstd, rstd


def norm_back(v, dy, gain):
    xhat, rstd = stats(v)
    dx = dy * gain
    m1 = jnp.mean(dx, axis=-1, keepdims=True)
    m2 = jnp.mean(dx * xhat, axis=-1, keepdims=True)
    return (dx - m1 - xhat * m2) * rstd, jnp.sum(dy * xhat, axis=0, keepdims=True), jnp.sum(dy, axis=0, keepdims=True)


ORDERS = (((0, 1, 2), 0), ((1, 0, 2), 2))
LAGS = ((1, 2, 2, 1, 1, 1, 1, 2), (1, 2, 1, 1, 1, 1, 1, 2))
EVERY, OFFSET = 4, 3


def reduce_plan(n_clips, which):
    bits = n_clips.bit_length() - 1
    first, side_at = ORDERS[which]
    order = [b for b in first if b < bits] + list(range(3, bits))
    plan = [("core", 0, CHUNK, False)]
    rows = CHUNK
    gathers = []
    for n, bit in enumerate(order):
        if n == side_at:
            plan.append(("side", 0, rows, False))
        halving = rows >= 32
        if halving:
            rows //= 2
            gathers.append(("gather", bit, rows, True))
        plan.append(("reduce", bit, rows, halving))
    return plan, plan + gathers[::-1]


def layer_kernel(dims, n_clips, count_ref, tok_ref, ext_ref, og_ref, proj_ref, qkv_ref, up_ref, down_ref,
                 gain1_ref, bias1_ref, gain2_ref, bias2_ref, projb_ref, downb_ref, upb_ref, qvb_ref, table_ref,
                 grad_ref, upg_ref, small_ref, res_ref, ing_ref,
                 w, tokb, extb, ogb, qvb, upb, stream, first, qkvt, probs, mixed, middle, second, ff, sg, branch, outp,
                 inp, core_buf, side_buf, land_a, land_c, small, small_buf, l_sem, t_sem, y_sem, q_sem, f_sem, c_sem,
                 r_sem, s_sem, o_sem):
    here, slots, width, hidden, features = dims
    bits = n_clips.bit_length() - 1
    c = lax.axis_index("clips")
    t = lax.axis_index("tp")
    k, u = bit_of(t, 1), bit_of(t, 2)
    core = (c, flip(t, 1))
    side = (c, flip(t, 2))
    across = (flip(c, 1), t)
    along = (flip(c, 2), t)
    others = [(c, lax.rem(t + i, N_TP)) for i in range(1, N_TP)]
    peers = [(flip(c, 2 ** bit), t) for bit in range(bits)]
    c_bits = [bit_of(c, 2 ** bit) for bit in range(bits)]
    own_slots = slots // N_TP
    n_rows = here * slots
    nf = hidden // F_BLOCK
    n_chunks = 3 * features // CHUNK
    b0, b1 = bit_of(c, 1), bit_of(c, 2)
    quarter = b1 * 2 + b0
    via_z = (1 - b1) * 2 + b0
    via_x = b1 * 2 + (1 - b0)
    blocks = [(0, 1, F_BLOCK * j, F_BLOCK) for j in range(features // F_BLOCK)] + [
        (1, 2, F_BLOCK * j, F_BLOCK) for j in range(nf)]
    na = features // F_BLOCK
    nb = len(blocks)
    half = features // 2
    tiles = features // F_BLOCK

    def weights_in():
        copies = [pltpu.make_async_copy(qkv_ref, w.at[u, k, 0, pl.ds(0, 3 * width)], l_sem.at[0]),
                  pltpu.make_async_copy(proj_ref, w.at[u, k, 0, pl.ds(3 * width, width)], l_sem.at[1]),
                  pltpu.make_async_copy(down_ref, w.at[u, k, 2], l_sem.at[2])]
        for i in range(tiles):
            for j in range(nf):
                copies.append(pltpu.make_async_copy(
                    up_ref.at[pl.ds(F_BLOCK * i, F_BLOCK), pl.ds(F_BLOCK * j, F_BLOCK)], probs.at[0, i * nf + j],
                    l_sem.at[3 + i * nf + j]))
        return copies

    def row_copies():
        mine = pl.ds(t * here, here)
        cols = pl.ds(t * own_slots, own_slots)
        return [pltpu.make_async_copy(tok_ref.at[mine], tokb.at[:, cols], o_sem.at[0, 2, 0]),
                pltpu.make_async_copy(og_ref.at[mine], ogb.at[:, cols], o_sem.at[0, 2, 1]),
                pltpu.make_async_copy(ext_ref, extb.at[t], o_sem.at[0, 2, 2]),
                pltpu.make_async_copy(qvb_ref, qvb.at[t], o_sem.at[1, 2, 0])]

    own_w = weights_in()
    for copy in own_w + row_copies():
        copy.start()

    barrier = pltpu.get_barrier_semaphore()
    targets = others + peers
    for target in targets:
        pl.semaphore_signal(barrier, inc=1, device_id=target, device_id_type=MESH)
    pl.semaphore_wait(barrier, len(targets))

    def remote(src, dst, sem, index, target):
        return pltpu.make_async_remote_copy(src_ref=src, dst_ref=dst, send_sem=sem.at[(0, *index)],
                                            recv_sem=sem.at[(1, *index)], device_id=target, device_id_type=MESH)

    def rows_copy(n, i):
        target = others[i]
        mine = pl.ds(target[1] * here, here)
        cols = pl.ds(t * own_slots, own_slots)
        src, dst = (lambda: (tok_ref.at[mine], tokb.at[:, cols]), lambda: (ext_ref, extb.at[t]),
                    lambda: (og_ref.at[mine], ogb.at[:, cols]), lambda: (qvb_ref, qvb.at[t]),
                    lambda: (upb.at[t], upb.at[t]))[n]()
        return remote(src, dst, t_sem, (n, i), target)

    def w_copy(kind, i):
        part, parts, base, rows = blocks[i]
        q, h = rows // 4, rows // 8
        su, start, size, sem, index, target = {
            "y": (u, base + quarter * q, q, y_sem, (i,), side),
            "x": (1 - u, base + quarter * q, q, q_sem, (0, i), across),
            "z": (1 - u, base + quarter * q, q, q_sem, (1, i), along),
            "xf": (1 - u, base + via_z * q, h, f_sem, (0, i), across),
            "zf": (1 - u, base + via_x * q + h, h, f_sem, (1, i), along),
            "co": (u, base, rows, c_sem, (0, i), core),
            "cf": (1 - u, base, rows, c_sem, (1, i), core),
        }[kind]
        view = w.at[su, k, pl.ds(part, parts), pl.ds(aligned(start), size)]
        return remote(view, view, sem, index, target)

    def step1(i):
        w_copy("y", i).wait_recv()
        w_copy("x", i).start()
        w_copy("z", i).start()

    def step2(i):
        w_copy("z", i).wait_recv()
        w_copy("xf", i).start()
        w_copy("x", i).wait_recv()
        w_copy("zf", i).start()

    def step3(i):
        w_copy("xf", i).wait_recv()
        w_copy("zf", i).wait_recv()
        w_copy("cf", i).start()

    def step4(i):
        w_copy("co", i).wait_recv()
        w_copy("cf", i).wait_recv()
        for kind in ("y", "x", "z", "xf", "zf", "co", "cf"):
            w_copy(kind, i).wait_send()

    def start_rows(n):
        for i in range(N_TP - 1):
            rows_copy(n, i).start()

    def wait_rows(n):
        for i in range(N_TP - 1):
            rows_copy(n, i).wait_recv()

    upb[pl.ds(t, 1), :, :] = row(upb_ref).reshape(1, 1, hidden)
    own_w[0].wait()
    for i in range(na):
        if i == na - 1:
            own_w[1].wait()
        w_copy("y", i).start()
    for n in (1, 3, 4):
        start_rows(n)
    for i in range(na):
        w_copy("co", i).start()
    for copy in own_w[2:]:
        copy.wait()
    for i in range(tiles):
        for j in range(nf):
            w[u, k, 1, j * F_BLOCK : (j + 1) * F_BLOCK, i * F_BLOCK : (i + 1) * F_BLOCK] = probs[0, i * nf + j].T
    for copy in row_copies():
        copy.wait()

    step1(0)
    start_rows(0)
    small[...] = jnp.zeros_like(small)
    step1(1)
    step2(0)
    step1(2)
    w_copy("y", na).start()
    ff[...] = jnp.zeros_like(ff)
    sg[...] = jnp.zeros_like(sg)
    step2(1)
    step2(2)
    w_copy("y", na + 1).start()
    for i in range(na):
        step3(i)
    for n in (1, 3, 4, 0):
        wait_rows(n)
    start_rows(2)

    per_clip = slots // ROWS
    sources = ROWS // own_slots

    def rows_at(i):
        return lax.div(i, per_clip), pl.ds(pl.multiple_of(lax.rem(i, per_clip) * ROWS, ROWS), ROWS), pl.ds(
            pl.multiple_of(i * ROWS, ROWS), ROWS)

    def first_rows(i, _):
        b, here_rows, rows = rows_at(i)
        line = lax.broadcasted_iota(jnp.int32, (2 * TABLE, own_slots), 0) & (TABLE - 1)
        pos = []
        for n in range(sources):
            place = extb[lax.rem(i, per_clip) * sources + n, pl.ds(t * here + b, 1), :]
            hot = [jnp.where(line == lax.broadcast_in_dim(v, line.shape, (0, 1)), 1.0, 0.0).astype(BF)
                   for v in (lax.shift_right_logical(place, 6), place & (TABLE - 1))]
            hi = dot(hot[0], table_ref[0 : 2 * TABLE, :], TN)
            lo = dot(hot[1], table_ref[2 * TABLE :, :], TN)
            sh, ch, sl, cl = hi[:, :half], hi[:, half:], lo[:, :half], lo[:, half:]
            pos.append(jnp.concatenate([sh * cl + ch * sl, ch * cl - sh * sl], axis=1))
        v = tokb[b, here_rows, :].astype(F32) + jnp.concatenate(pos, axis=0)
        stream[rows, :] = v
        xhat, _ = stats(v)
        first[rows, :] = (xhat * row(gain1_ref) + row(bias1_ref)).astype(BF)
        return 0

    lax.fori_loop(0, n_rows // ROWS, first_rows, 0)
    for i in range(na):
        step4(i)
    for i in range(na, nb):
        w_copy("co", i).start()

    scale = HD ** -0.5

    def qkv_of(g, _):
        gu, gk = lax.div(g, 2), lax.rem(g, 2)
        out = dot(w[gu, gk, 0, 0 : 3 * width, :], first[...], NT)
        add = jnp.concatenate([qvb[g, :, :], jnp.zeros((6, width), F32)], axis=0)
        add = jnp.concatenate([add, jnp.zeros((8, 64), F32)], axis=1).T
        qkvt[g, 0:width, :] = ((out[0:width] + add[0:width, 0:1]).astype(BF).astype(F32) * scale).astype(BF)
        qkvt[g, width : 2 * width, :] = out[width : 2 * width].astype(BF)
        qkvt[g, 2 * width :, :] = (out[2 * width :] + add[0:width, 1:2]).astype(BF)

        @pl.when(g == 1)
        def _():
            step1(na)
            w_copy("y", na + 2).start()

        return 0

    lax.fori_loop(0, N_TP, qkv_of, 0)

    per_group = width // HD

    def attend(g, _):
        for b in range(here):
            cols = slice(b * slots, (b + 1) * slots)
            visible = count_ref[t * here + b]
            keep = lax.broadcasted_iota(jnp.int32, (slots, slots), 0) < visible
            for r in range(per_group):
                q = qkvt[g, r * HD : (r + 1) * HD, cols]
                key = qkvt[g, width + r * HD : width + (r + 1) * HD, cols]
                value = qkvt[g, 2 * width + r * HD : 2 * width + (r + 1) * HD, cols]
                s = jnp.where(keep, dot(key, q, TN), NEGATIVE)
                e = jnp.exp(s - jnp.max(s, axis=0, keepdims=True))
                p = (e * (1.0 / jnp.sum(e, axis=0, keepdims=True))).astype(BF)
                probs[b, g * per_group + r] = p
                mixed[g, r * HD : (r + 1) * HD, cols] = dot(value, p, NN).astype(BF)

        @pl.when(g == 1)
        def _():
            step1(na + 1)

        @pl.when(g == 2)
        def _():
            step2(na)

        return 0

    lax.fori_loop(0, N_TP, attend, 0)
    step3(na)

    def second_rows(i, _):
        _, _, rows = rows_at(i)
        total = stream[rows, :] + row(projb_ref)
        for g in range(N_TP):
            total = total + dot(mixed[g, :, rows], w[g // 2, g % 2, 0, 3 * width :, :], TN)
        middle[rows, :] = total
        xhat, _ = stats(total)
        second[rows, :] = (xhat * row(gain2_ref) + row(bias2_ref)).astype(BF)
        return 0

    lax.fori_loop(0, n_rows // ROWS, second_rows, 0)
    step4(na)
    wait_rows(2)

    plans = [reduce_plan(n_clips, n) for n in (0, 1)]
    lands = (land_a, land_c)
    f_chunks = nf * 2 * F_BLOCK // CHUNK
    per_f = F_BLOCK // CHUNK

    def place_of(chunk):
        last = div(chunk, f_chunks)
        in_block = mod(chunk, 2 * per_f)
        part = (1 - last) * (1 + div(in_block, per_f))
        row = (1 - last) * (div(chunk, 2 * per_f) * F_BLOCK + mod(in_block, per_f) * CHUNK)
        return part, row + last * (chunk - f_chunks) * CHUNK

    def kept(which, stage):
        start = 0
        for kind, bit, rows, halving in plans[which][0][:stage]:
            if halving:
                start = start + c_bits[bit] * rows
        return start

    def copy_of(which, stage, chunk):
        kind, bit, rows, halving = plans[which][1][stage]
        both = ("side", 0) not in [p[:2] for p in plans[which][1][:stage]]
        base = chunk * CHUNK
        if kind == "core":
            part, row = place_of(chunk)
            src = w.at[:, 1 - k, part, pl.ds(aligned(row), CHUNK)]
            dst, target = core_buf.at[:, pl.ds(aligned(base), CHUNK)], core
        elif kind == "side":
            start = aligned(base + kept(which, stage))
            src, dst, target = core_buf.at[1 - u, pl.ds(start, rows)], side_buf.at[pl.ds(start, rows)], side
        elif kind == "reduce":
            start = base + kept(which, stage)
            if halving:
                start = start + (1 - c_bits[bit]) * rows
            at = pl.ds(aligned(land_at(which, stage, chunk)), rows)
            if both:
                src, dst = core_buf.at[:, pl.ds(aligned(start), rows)], lands[which].at[:, at]
            else:
                src, dst = side_buf.at[pl.ds(aligned(start), rows)], lands[which].at[0, at]
            target = peers[bit]
        else:
            depth = [p[:2] for p in plans[which][0]].index(("reduce", bit))
            part, row = place_of(chunk)
            src = grad_ref.at[part, pl.ds(aligned(row + kept(which, depth + 1)), rows)]
            dst, target = src, peers[bit]
        send = chunk if kind == "reduce" and not halving else which
        return pltpu.make_async_remote_copy(
            src_ref=src, dst_ref=dst, send_sem=r_sem.at[0, stage, send], recv_sem=r_sem.at[1, stage, chunk],
            device_id=target, device_id_type=MESH)

    def land_at(which, stage, chunk):
        at = 0
        for kind, bit, rows, halving in plans[which][0][:stage]:
            if kind == "reduce":
                at += rows
        size = sum(p[2] for p in plans[which][0] if p[0] == "reduce")
        index = div(chunk, EVERY)
        if which == 0:
            index = index * (EVERY - 1) + mod(mod(chunk, EVERY) + EVERY - OFFSET - 1, EVERY)
        return index * size + at

    def add(a, b):
        return (a.astype(F32) + b.astype(F32)).astype(BF)

    def finish(which, stage, chunk):
        copy_of(which, stage, chunk).wait_recv()
        kind, bit, rows, halving = plans[which][1][stage]
        both = ("side", 0) not in [p[:2] for p in plans[which][1][:stage]]
        base = chunk * CHUNK
        last = stage == len(plans[which][0]) - 1
        if kind == "core":
            part, row = place_of(chunk)
            at = pl.ds(aligned(base), CHUNK)
            for n in (0, 1):
                core_buf[n, at] = add(w[n, k, part, pl.ds(aligned(row), CHUNK)], core_buf[n, at])
        elif kind == "side":
            at = pl.ds(aligned(base + kept(which, stage)), rows)
            side_buf[at] = add(core_buf[u, at], side_buf[at])
        elif kind == "reduce":
            at = pl.ds(aligned(base + kept(which, stage + 1)), rows)
            land = pl.ds(aligned(land_at(which, stage, chunk)), rows)
            if not halving:
                copy_of(which, stage, chunk).wait_send()
            if both:
                for n in (0, 1):
                    core_buf[n, at] = add(core_buf[n, at], lands[which][n, land])
            elif last:
                part, row = place_of(chunk)
                grad_ref[part, pl.ds(aligned(row + kept(which, stage + 1)), rows)] = add(
                    side_buf[at], lands[which][0, land])
            else:
                side_buf[at] = add(side_buf[at], lands[which][0, land])

    starts = []
    for which in (0, 1):
        lags = list(LAGS[which]) + [1] * 32
        starts.append([sum(lags[:n]) for n in range(len(plans[which][1]) + 1)])

    def step(which, stage, chunk):
        if stage > 0:
            finish(which, stage - 1, chunk)
        if stage < len(plans[which][1]):
            copy_of(which, stage, chunk).start()

    def tick(i):
        for which in (0, 1):
            for stage in range(len(plans[which][1]) + 1):
                chunk = i - starts[which][stage]
                mine = lax.rem(chunk + EVERY, EVERY) == OFFSET
                if which == 0:
                    mine = jnp.logical_not(mine)

                @pl.when((chunk >= 0) & (chunk < n_chunks) & mine)
                def _():
                    step(which, stage, chunk)

    def ffn(i, _):
        j, g = lax.div(i, N_TP), lax.rem(i, N_TP)
        gu, gk = lax.div(g, 2), lax.rem(g, 2)
        for at, work in ((0, lambda: step2(na + 1)), (1, lambda: step1(na + 2)), (2, lambda: step3(na + 1)),
                         (3, lambda: step2(na + 2)), (4, lambda: step4(na + 1)), (6, lambda: step3(na + 2)),
                         (8, lambda: step4(na + 2))):
            @pl.when(i == at)
            def _():
                work()

        hid = pl.ds(pl.multiple_of(j * F_BLOCK, F_BLOCK), F_BLOCK)
        up, down = w[gu, gk, 1, hid, :], w[gu, gk, 2, hid, :]
        pre = dot(second[...], up, NT) + upb[g, :, hid]
        act, slope = gelu_parts(pre)
        act = act.astype(BF)
        ff[...] += dot(act, down, NN)
        og = ogb[...].reshape(n_rows, features)
        pg = (dot(og, down, NT) * slope).astype(BF)
        sg[...] += dot(pg, up, NN)
        w[gu, gk, 2, hid, :] = dot(act, og, TN).astype(BF)
        w[gu, gk, 1, hid, :] = dot(pg, second[...], TN).astype(BF)
        small[pl.ds(8 + g, 1), hid] = jnp.sum(pg.astype(F32), axis=0, keepdims=True)

        @pl.when(i >= N_TP)
        def _():
            tick(i - N_TP)

        return 0

    lax.fori_loop(0, nf * N_TP, ffn, 0)
    done = (nf - 1) * N_TP

    def middle_rows(i, _):
        b, here_rows, rows = rows_at(i)
        m = middle[rows, :]
        outp[b, here_rows, :] = (m + ff[rows, :] + row(downb_ref)).astype(BF)
        dv, dgain, dbias = norm_back(m, sg[rows, :], row(gain2_ref))
        og = ogb[b, here_rows, :].astype(F32)
        mg = og + dv
        ff[rows, :] = mg
        bg = mg.astype(BF)
        branch[rows, :] = bg
        small[2:3, :] += dgain
        small[3:4, :] += dbias
        small[4:5, :] += jnp.sum(bg.astype(F32), axis=0, keepdims=True)
        small[5:6, :] += jnp.sum(og, axis=0, keepdims=True)
        return 0

    lax.fori_loop(0, n_rows // ROWS, middle_rows, 0)

    def back_copy(n, i):
        src, dst = ((outp, res_ref), (inp, ing_ref))[n]
        target = others[i]
        return remote(src.at[:, pl.ds(target[1] * own_slots, own_slots)], dst.at[pl.ds(t * here, here)], o_sem,
                      (n, i), target)

    def back_own(n):
        src, dst = ((outp, res_ref), (inp, ing_ref))[n]
        return pltpu.make_async_copy(src.at[:, pl.ds(t * own_slots, own_slots)], dst.at[pl.ds(t * here, here)],
                                     l_sem.at[n])

    def send_back(n):
        back_own(n).start()
        for i in range(N_TP - 1):
            back_copy(n, i).start()

    send_back(0)
    sg[...] = jnp.zeros_like(sg)

    def back_group(g, _):
        gu, gk = lax.div(g, 2), lax.rem(g, 2)
        bg = branch[...]
        dmix = dot(w[gu, gk, 0, 3 * width :, :], bg, NT).astype(BF)
        w[gu, gk, 0, 3 * width :, :] = dot(mixed[g], bg, NN).astype(BF)
        for b in range(here):
            cols = slice(b * slots, (b + 1) * slots)
            for r in range(per_group):
                q_rows = slice(r * HD, (r + 1) * HD)
                k_rows = slice(width + r * HD, width + (r + 1) * HD)
                v_rows = slice(2 * width + r * HD, 2 * width + (r + 1) * HD)
                q, key, value = qkvt[g, q_rows, cols], qkvt[g, k_rows, cols], qkvt[g, v_rows, cols]
                dm = dmix[q_rows, cols]
                p = probs[b, g * per_group + r]
                pf = p.astype(F32)
                dp = dot(value, dm, TN)
                ds = (pf * (dp - jnp.sum(pf * dp, axis=0, keepdims=True))).astype(BF)
                qkvt[g, q_rows, cols] = (dot(key, ds, NN) * scale).astype(BF)
                qkvt[g, k_rows, cols] = dot(q, ds, NT).astype(BF)
                qkvt[g, v_rows, cols] = dot(dm, p, NT).astype(BF)
        dqkv = qkvt[g]
        sg[...] += dot(dqkv, w[gu, gk, 0, 0 : 3 * width, :], TN)
        w[gu, gk, 0, 0 : 3 * width, :] = dot(dqkv, first[...], NN).astype(BF)
        small[pl.ds(12 + g, 1), 0 : 3 * width] = dot(jnp.ones((8, n_rows), BF), dqkv, NT)[0:1]
        tick(done + g)
        return 0

    lax.fori_loop(0, N_TP, back_group, 0)

    def last_rows(i, _):
        b, here_rows, rows = rows_at(i)
        dv, dgain, dbias = norm_back(stream[rows, :], sg[rows, :], row(gain1_ref))
        inp[b, here_rows, :] = (ff[rows, :] + dv).astype(BF)
        small[0:1, :] += dgain
        small[1:2, :] += dbias
        return 0

    lax.fori_loop(0, n_rows // ROWS, last_rows, 0)
    send_back(1)

    small_targets = [core, side] + peers

    def small_copy(i):
        return remote(small, small_buf.at[i], s_sem, (i,), small_targets[i])

    done = done + N_TP

    def rest_of(i, _):
        tick(i)
        return 0

    lax.fori_loop(done, n_chunks, rest_of, 0)
    state = {}
    for chunk in range(n_chunks):
        which = int(chunk % EVERY == OFFSET)
        n_all = len(plans[which][1])
        stage = max(n for n in range(n_all + 1) if chunk + starts[which][n] < n_chunks)
        if stage < n_all:
            state[chunk] = (which, stage)
    turn = 0
    up_left = True
    while state or turn <= len(small_targets):
        if turn <= len(small_targets):
            if turn > 0:
                small_copy(turn - 1).wait()
                small[...] += small_buf[turn - 1]
            if turn < len(small_targets):
                small_copy(turn).start()
        for chunk in sorted(state):
            which, stage = state[chunk]
            step(which, stage + 1, chunk)
            state[chunk] = (which, stage + 1)
            if stage + 1 == len(plans[which][1]):
                del state[chunk]
        if up_left and not [chunk for chunk in state if chunk < f_chunks]:
            up_left = False
            for m in range(tiles):
                for j in range(nf):
                    upg_ref[m * F_BLOCK : (m + 1) * F_BLOCK, j * F_BLOCK : (j + 1) * F_BLOCK] = grad_ref[
                        1, j * F_BLOCK : (j + 1) * F_BLOCK, m * F_BLOCK : (m + 1) * F_BLOCK].T
        turn += 1
    small_ref[0:6, :] = small[0:6, :]
    small_ref[6:7, :] = small[pl.ds(8 + t, 1), :]
    small_ref[7:8, :] = small[pl.ds(12 + t, 1), :]

    for n in (0, 1):
        for i in range(N_TP - 1):
            back_copy(n, i).wait_recv()
            back_copy(n, i).wait_send()
        back_own(n).wait()
    for n in range(5):
        for i in range(N_TP - 1):
            rows_copy(n, i).wait_send()

    for which in (0, 1):
        count = len([chunk for chunk in range(n_chunks) if (chunk % EVERY == OFFSET) == bool(which)])
        for stage, (kind, _, rows, halving) in enumerate(plans[which][1]):
            if kind != "reduce" or halving:
                both = ("side", 0) not in [p[:2] for p in plans[which][1][:stage]]
                view = core_buf.at[:, pl.ds(0, count * rows)] if both and kind != "side" else side_buf.at[
                    pl.ds(0, count * rows)]
                pltpu.make_async_remote_copy(
                    src_ref=view, dst_ref=view, send_sem=r_sem.at[0, stage, which], recv_sem=r_sem.at[1, stage, which],
                    device_id=core, device_id_type=MESH).wait_send()


def layer_call(n_clips, counts, tok, ext, og, proj, qkv, up, down, vectors, qv_bias, table):
    count, own_slots, features = tok.shape
    width = proj.shape[0]
    hidden = up.shape[1]
    here = count // N_TP
    slots = own_slots * N_TP
    n_rows = here * slots
    nf = hidden // F_BLOCK
    n_chunks = 3 * features // CHUNK
    heads = features // HD
    bits = n_clips.bit_length() - 1
    sizes = [sum(p[2] for p in reduce_plan(n_clips, n)[0] if p[0] == "reduce") for n in (0, 1)]
    n_all = max(len(reduce_plan(n_clips, n)[1]) for n in (0, 1))
    n_second = -(-n_chunks // EVERY)
    hbm = pl.BlockSpec(memory_space=pl.ANY)
    vmem = pl.BlockSpec(memory_space=pltpu.VMEM)
    smem = pl.BlockSpec(memory_space=pltpu.SMEM)
    dma = pltpu.SemaphoreType.DMA
    nb = nf + features // F_BLOCK
    return pl.pallas_call(
        functools.partial(layer_kernel, (here, slots, width, hidden, features), n_clips),
        out_shape=(
            jax.ShapeDtypeStruct((3, features, features), BF),
            jax.ShapeDtypeStruct((features, hidden), BF),
            jax.ShapeDtypeStruct((8, features), F32),
            jax.ShapeDtypeStruct((count, own_slots, features), BF),
            jax.ShapeDtypeStruct((count, own_slots, features), BF),
        ),
        in_specs=[smem, hbm, vmem] + [hbm] * 5 + [vmem] * 9,
        out_specs=(vmem, vmem, vmem, hbm, hbm),
        scratch_shapes=[
            pltpu.VMEM((2, 2, 3, features, features), BF),
            pltpu.VMEM((here, slots, features), BF),
            pltpu.VMEM((N_TP, *ext.shape), jnp.int32),
            pltpu.VMEM((here, slots, features), BF),
            pltpu.VMEM((N_TP, *qv_bias.shape), F32),
            pltpu.VMEM((N_TP, 1, hidden), F32),
            pltpu.VMEM((n_rows, features), F32),
            pltpu.VMEM((n_rows, features), BF),
            pltpu.VMEM((N_TP, 3 * width, n_rows), BF),
            pltpu.VMEM((here, heads, slots, slots), BF),
            pltpu.VMEM((N_TP, width, n_rows), BF),
            pltpu.VMEM((n_rows, features), F32),
            pltpu.VMEM((n_rows, features), BF),
            pltpu.VMEM((n_rows, features), F32),
            pltpu.VMEM((n_rows, features), F32),
            pltpu.VMEM((n_rows, features), BF),
            pltpu.VMEM((here, slots, features), BF),
            pltpu.VMEM((here, slots, features), BF),
            pltpu.VMEM((2, 3 * features, features), BF),
            pltpu.VMEM((3 * features, features), BF),
            pltpu.VMEM((1, n_second * (EVERY - 1) * sizes[0], features), BF),
            pltpu.VMEM((2, n_second * sizes[1], features), BF),
            pltpu.VMEM((16, features), F32),
            pltpu.VMEM((2 + bits, 16, features), F32),
            dma((3 + nf * features // F_BLOCK,)),
            dma((2, 5, N_TP - 1)),
            dma((2, nb)),
            dma((2, 2, nb)),
            dma((2, 2, nb)),
            dma((2, 2, nb)),
            dma((2, n_all, n_chunks)),
            dma((2, 2 + bits)),
            dma((2, 3, N_TP - 1)),
        ],
        compiler_params=pltpu.CompilerParams(collective_id=0, has_side_effects=True, vmem_limit_bytes=VMEM_LIMIT),
        name="encoder_layer",
    )(counts, tok, ext, og, proj, qkv, up, down, *vectors, qv_bias, table)


def widen_kernel(qkv_ref, proj_ref, down_ref, up_ref, out_ref, in_ref, small_ref, qkvo_ref, projo_ref, downo_ref,
                 upo_ref, outo_ref, ino_ref, qvo_ref, g1_ref, b1_ref, g2_ref, b2_ref, pb_ref, db_ref, ub_ref):
    for src, dst in ((qkv_ref, qkvo_ref), (proj_ref, projo_ref), (down_ref, downo_ref)):
        dst[...] = src[0].astype(F32)
    for src, dst in ((up_ref, upo_ref), (out_ref, outo_ref), (in_ref, ino_ref)):
        dst[...] = src[...].astype(F32)
    width = qvo_ref.shape[1]

    @pl.when(pl.program_id(0) == 0)
    def _():
        for i, ref in enumerate((g1_ref, b1_ref, g2_ref, b2_ref, pb_ref, db_ref, ub_ref)):
            ref[...] = small_ref[i, :]
        qvo_ref[0:1, :] = small_ref[7:8, 0:width]
        qvo_ref[1:2, :] = small_ref[7:8, 2 * width : 3 * width]


def widen_call(grads, up_grad, small, rows_out, rows_in, width):
    _, features, _ = grads.shape
    hidden = up_grad.shape[1]
    count, own_slots, _ = rows_out.shape
    steps = 4
    whole = pl.BlockSpec(memory_space=pltpu.VMEM)

    def rows_of(rows, first):
        return pl.BlockSpec((1, rows // steps, features), lambda i: (first[0], first[1] // (rows // steps) + i, 0))

    def flat(rows, cols):
        return pl.BlockSpec((rows // steps, cols), lambda i: (i, 0))

    clips = pl.BlockSpec((count // steps, own_slots, features), lambda i: (i, 0, 0))
    vector = jax.ShapeDtypeStruct((features,), F32)
    return pl.pallas_call(
        widen_kernel,
        grid=(steps,),
        out_shape=(
            jax.ShapeDtypeStruct((3 * width, features), F32),
            jax.ShapeDtypeStruct((width, features), F32),
            jax.ShapeDtypeStruct((hidden, features), F32),
            jax.ShapeDtypeStruct((features, hidden), F32),
            jax.ShapeDtypeStruct((count, own_slots, features), F32),
            jax.ShapeDtypeStruct((count, own_slots, features), F32),
            jax.ShapeDtypeStruct((2, width), F32),
        ) + (vector,) * 6 + (jax.ShapeDtypeStruct((hidden,), F32),),
        in_specs=[rows_of(3 * width, (0, 0)), rows_of(width, (0, 3 * width)), rows_of(hidden, (2, 0)),
                  flat(features, hidden), clips, clips, whole],
        out_specs=(flat(3 * width, features), flat(width, features), flat(hidden, features), flat(features, hidden),
                   clips, clips) + (whole,) * 8,
        compiler_params=pltpu.CompilerParams(vmem_limit_bytes=VMEM_LIMIT),
        name="widen",
    )(grads, grads, grads, up_grad, rows_out, rows_in, small)


def place_table(features, largest):
    half = features // 2
    freq = np.exp(-math.log(10000.0) * np.arange(half, dtype=np.float64) / half).astype(np.float32).astype(np.float64)
    parts = []
    for step in (TABLE, 1):
        angle = step * np.arange(TABLE, dtype=np.float64)[:, None] * freq
        values = np.concatenate([np.sin(angle), np.cos(angle)], axis=1).astype(np.float32)
        high = values.astype(BF)
        parts += [high, (values - high.astype(np.float32)).astype(BF)]
    return np.concatenate(parts, axis=0)


def per_device(n_clips, tokens, tubelet_index, visible_count, norm1_gain, norm1_bias, qkv_weight, qv_bias,
               proj_weight, proj_bias, norm2_gain, norm2_bias, up_weight, up_bias, down_weight, down_bias, out_grad):
    count, rows, features = tokens.shape
    width = qkv_weight.shape[2]
    hidden = up_weight.shape[1]
    qkv_t = jnp.transpose(qkv_weight, (1, 2, 0)).reshape(3 * width, features)
    vectors = (norm1_gain, norm1_bias, norm2_gain, norm2_bias, proj_bias, down_bias, up_bias)
    table = jnp.asarray(place_table(features, 2560))
    grads, up_grad, small, rows_out, rows_in = layer_call(
        n_clips, visible_count, tokens, tubelet_index, out_grad, proj_weight, qkv_t, up_weight, down_weight, vectors, qv_bias,
        table)
    qkv_grad, proj_grad, down_grad, up_grad, rows_out, rows_in, qv_grad, g1, b1, g2, b2, pb, db, ub = widen_call(
        grads, up_grad, small, rows_out, rows_in, width)
    qkv_grad = jnp.transpose(qkv_grad.reshape(3, width, features), (2, 0, 1))
    return rows_out, rows_in, g1, b1, qkv_grad, qv_grad, proj_grad, pb, g2, b2, up_grad, ub, down_grad, db


def solution(mesh):
    placed = (
        P("clips", "tp", None), P("clips", "tp"), P("clips"), P(), P(), P(None, None, "tp"), P(None, "tp"),
        P("tp", None), P(), P(), P(), P(None, "tp"), P("tp"), P("tp", None), P(), P("clips", "tp", None),
    )
    return jax.shard_map(
        functools.partial(per_device, mesh.shape["clips"]),
        mesh=mesh,
        in_specs=placed,
        out_specs=(
            P("clips", "tp", None), P("clips", "tp", None), P(), P(), P(None, None, "tp"), P(None, "tp"),
            P("tp", None), P(), P(), P(), P(None, "tp"), P("tp"), P("tp", None), P(),
        ),
        check_vma=False,
    )
```

time: 225 us -> 188 us (0.84)
  local copies, waits for them, and re-layouts: 17.8 us -> 0 us
  Pallas kernels: 201 us -> 187 us
  other arithmetic: 4.74 us -> 0 us
    pallas_call x1, Pallas kernels: 201 us -> 181 us  [layer_call(): pl.pallas_call(functools.partial(layer_kernel, (here, slots, width, hidde...]
    slice x7 -> x0, local copies, waits for them, and re-layouts: 10.2 us -> none  [the longest x1 2.76 us: per_device(): ffn_grad[:, 1].reshape(hidden, features)]
    pallas_call x0 -> x1, Pallas kernels: none -> 6.9 us  [widen_call(): pl.pallas_call(widen_kernel, grid=(steps,), out_shape=(jax.ShapeDtypeStru...]
    unnamed x20 -> x0, local copies, waits for them, and re-layouts: 5.6 us -> none
    convert_element_type x3 -> x0, other arithmetic: 3.28 us -> none  [the longest x1 1.28 us: per_device(): rows_out.astype(F32)]
where the time goes in v1:
time: 188 us
  Pallas kernels  187 us (99%)
    pallas_call x1, Pallas kernels, layer_call(): pl.pallas_call(functools.partial(layer_kernel, (here, slots, width, hidde...  181 us
    pallas_call x1, Pallas kernels, widen_call(): pl.pallas_call(widen_kernel, grid=(steps,), out_shape=(jax.ShapeDtypeStru...  6.9 us

profile of v1, /device:TPU:0, one launch (start us, length us, event | category | flops | bytes accessed | tf_op | source)
XLA Modules:
  0.0 188.1 jit_solution(8408157402401413169)
XLA Ops:
  0.7 180.6 %encoder_layer.1 = (bf16[3,768,768]{2,1,0:T(8,128)(2,1)}, bf16[768,768]{1,0:T(8,128)(2,1)}, f32[8,768]{1,0:T(8,128)}, bf16[8,64,768]{2,1,0:T(8,128)(2,1)}, bf16[8,64,768]{2,1,0:T(8,128)(2,1)}) custom-call(s32[8]{0:T(128)} %count_ref.1, bf16[8,64,768]{2,1,0:T(8,128)(2,1)} %tok_ref.1, s32[8,64]{1,0:T(8,128)} %ext_ref.1, bf16[8,64,768]{2,1,0:T(8,128)(2,1)} %og_ref.1, ...), custom_call_target="tpu_custom_call" | custom-call | tf_op jit(solution)/shard_map/encoder_layer/pallas_call | solution.py:666
  181.2 6.9 %widen.1 = (f32[576,768]{1,0:T(8,128)}, f32[192,768]{1,0:T(8,128)}, f32[768,768]{1,0:T(8,128)}, f32[768,768]{1,0:T(8,128)}, f32[8,64,768]{2,1,0:T(8,128)}, /*ind...) custom-call(bf16[3,768,768]{2,1,0:T(8,128)(2,1)} %get-tuple-element., ...), custom_call_target="tpu_custom_call" | custom-call | tf_op jit(solution)/shard_map/widen/pallas_call | solution.py:748

commit v2 on v1

--- a/solution.py
+++ b/solution.py
@@ -79,21 +79,15 @@
     return (dx - m1 - xhat * m2) * rstd, jnp.sum(dy * xhat, axis=0, keepdims=True), jnp.sum(dy, axis=0, keepdims=True)
 
 
-ORDERS = (((0, 1, 2), 0), ((1, 0, 2), 2))
-LAGS = ((1, 2, 2, 1, 1, 1, 1, 2), (1, 2, 1, 1, 1, 1, 1, 2))
-EVERY, OFFSET = 4, 3
-
-
-def reduce_plan(n_clips, which):
-    bits = n_clips.bit_length() - 1
-    first, side_at = ORDERS[which]
-    order = [b for b in first if b < bits] + list(range(3, bits))
-    plan = [("core", 0, CHUNK, False)]
+LAGS = (1, 2, 2, 1, 1, 1, 1, 2)
+BACK = {("t", 2): [(n, piece) for n in (0, 1) for piece in range(4)]}
+
+
+def reduce_plan(n_clips):
+    plan = [("core", 0, CHUNK, False), ("side", 0, CHUNK, False)]
     rows = CHUNK
     gathers = []
-    for n, bit in enumerate(order):
-        if n == side_at:
-            plan.append(("side", 0, rows, False))
+    for bit in range(n_clips.bit_length() - 1):
         halving = rows >= 32
         if halving:
             rows //= 2
@@ -106,8 +100,8 @@
                  gain1_ref, bias1_ref, gain2_ref, bias2_ref, projb_ref, downb_ref, upb_ref, qvb_ref, table_ref,
                  grad_ref, upg_ref, small_ref, res_ref, ing_ref,
                  w, tokb, extb, ogb, qvb, upb, stream, first, qkvt, probs, mixed, middle, second, ff, sg, branch, outp,
-                 inp, core_buf, side_buf, land_a, land_c, small, small_buf, l_sem, t_sem, y_sem, q_sem, f_sem, c_sem,
-                 r_sem, s_sem, o_sem):
+                 inp, core_buf, side_buf, land, small, upsum, small_buf, l_sem, t_sem, y_sem, q_sem, f_sem, c_sem,
+                 r_sem, s_sem, o_sem, b_sem):
     here, slots, width, hidden, features = dims
     bits = n_clips.bit_length() - 1
     c = lax.axis_index("clips")
@@ -209,9 +203,13 @@
         w_copy("cf", i).start()
 
     def step4(i):
+        w_copy("cf", i).wait_recv()
+        for kind in ("x", "z", "xf", "zf", "cf"):
+            w_copy(kind, i).wait_send()
+
+    def step_own(i):
         w_copy("co", i).wait_recv()
-        w_copy("cf", i).wait_recv()
-        for kind in ("y", "x", "z", "xf", "zf", "co", "cf"):
+        for kind in ("y", "co"):
             w_copy(kind, i).wait_send()
 
     def start_rows(n):
@@ -252,8 +250,6 @@
     step2(1)
     step2(2)
     w_copy("y", na + 1).start()
-    for i in range(na):
-        step3(i)
     for n in (1, 3, 4, 0):
         wait_rows(n)
     start_rows(2)
@@ -285,14 +281,18 @@
 
     lax.fori_loop(0, n_rows // ROWS, first_rows, 0)
     for i in range(na):
-        step4(i)
+        step_own(i)
     for i in range(na, nb):
         w_copy("co", i).start()
 
     scale = HD ** -0.5
 
-    def qkv_of(g, _):
-        gu, gk = lax.div(g, 2), lax.rem(g, 2)
+    def group(n):
+        gu, gk = lax.rem(u + lax.div(n, 2), 2), lax.rem(n, 2)
+        return gu * 2 + gk, gu, gk
+
+    def qkv_of(n):
+        g, gu, gk = group(n)
         out = dot(w[gu, gk, 0, 0 : 3 * width, :], first[...], NT)
         add = jnp.concatenate([qvb[g, :, :], jnp.zeros((6, width), F32)], axis=0)
         add = jnp.concatenate([add, jnp.zeros((8, 64), F32)], axis=1).T
@@ -300,18 +300,22 @@
         qkvt[g, width : 2 * width, :] = out[width : 2 * width].astype(BF)
         qkvt[g, 2 * width :, :] = (out[2 * width :] + add[0:width, 1:2]).astype(BF)
 
-        @pl.when(g == 1)
+
+    per_group = width // HD
+
+    def attend(n, _):
+        @pl.when(n == 1)
         def _():
-            step1(na)
-            w_copy("y", na + 2).start()
-
-        return 0
-
-    lax.fori_loop(0, N_TP, qkv_of, 0)
-
-    per_group = width // HD
-
-    def attend(g, _):
+            for i in range(na):
+                step3(i)
+
+        @pl.when(n == 2)
+        def _():
+            for i in range(na):
+                step4(i)
+
+        qkv_of(n)
+        g, _, _ = group(n)
         for b in range(here):
             cols = slice(b * slots, (b + 1) * slots)
             visible = count_ref[t * here + b]
@@ -326,18 +330,15 @@
                 probs[b, g * per_group + r] = p
                 mixed[g, r * HD : (r + 1) * HD, cols] = dot(value, p, NN).astype(BF)
 
-        @pl.when(g == 1)
-        def _():
-            step1(na + 1)
-
-        @pl.when(g == 2)
-        def _():
-            step2(na)
+        for at, work in ((0, lambda: (step1(na), w_copy("y", na + 2).start())), (1, lambda: step1(na + 1)),
+                         (2, lambda: step2(na))):
+            @pl.when(n == at)
+            def _():
+                work()
 
         return 0
 
     lax.fori_loop(0, N_TP, attend, 0)
-    step3(na)
 
     def second_rows(i, _):
         _, _, rows = rows_at(i)
@@ -350,156 +351,143 @@
         return 0
 
     lax.fori_loop(0, n_rows // ROWS, second_rows, 0)
-    step4(na)
+    step3(na)
+    step_own(na)
     wait_rows(2)
 
-    plans = [reduce_plan(n_clips, n) for n in (0, 1)]
-    lands = (land_a, land_c)
+    sums, plan = reduce_plan(n_clips)
+    n_all = len(plan)
     f_chunks = nf * 2 * F_BLOCK // CHUNK
     per_f = F_BLOCK // CHUNK
 
     def place_of(chunk):
         last = div(chunk, f_chunks)
         in_block = mod(chunk, 2 * per_f)
-        part = (1 - last) * (1 + div(in_block, per_f))
-        row = (1 - last) * (div(chunk, 2 * per_f) * F_BLOCK + mod(in_block, per_f) * CHUNK)
+        part = (1 - last) * (1 + mod(in_block, 2))
+        row = (1 - last) * (div(chunk, 2 * per_f) * F_BLOCK + div(in_block, 2) * CHUNK)
         return part, row + last * (chunk - f_chunks) * CHUNK
 
-    def kept(which, stage):
+    def kept(stage):
         start = 0
-        for kind, bit, rows, halving in plans[which][0][:stage]:
+        for kind, bit, rows, halving in sums[:stage]:
             if halving:
                 start = start + c_bits[bit] * rows
         return start
 
-    def copy_of(which, stage, chunk):
-        kind, bit, rows, halving = plans[which][1][stage]
-        both = ("side", 0) not in [p[:2] for p in plans[which][1][:stage]]
+    def land_at(stage, chunk):
+        return chunk * sum(p[2] for p in sums[2:]) + sum(p[2] for p in sums[2:stage])
+
+    def copy_of(stage, chunk):
+        kind, bit, rows, halving = plan[stage]
         base = chunk * CHUNK
         if kind == "core":
             part, row = place_of(chunk)
             src = w.at[:, 1 - k, part, pl.ds(aligned(row), CHUNK)]
             dst, target = core_buf.at[:, pl.ds(aligned(base), CHUNK)], core
         elif kind == "side":
-            start = aligned(base + kept(which, stage))
-            src, dst, target = core_buf.at[1 - u, pl.ds(start, rows)], side_buf.at[pl.ds(start, rows)], side
+            at = pl.ds(aligned(base), rows)
+            src, dst, target = core_buf.at[1 - u, at], side_buf.at[at], side
         elif kind == "reduce":
-            start = base + kept(which, stage)
+            start = base + kept(stage)
             if halving:
                 start = start + (1 - c_bits[bit]) * rows
-            at = pl.ds(aligned(land_at(which, stage, chunk)), rows)
-            if both:
-                src, dst = core_buf.at[:, pl.ds(aligned(start), rows)], lands[which].at[:, at]
-            else:
-                src, dst = side_buf.at[pl.ds(aligned(start), rows)], lands[which].at[0, at]
-            target = peers[bit]
+            src = side_buf.at[pl.ds(aligned(start), rows)]
+            dst, target = land.at[pl.ds(aligned(land_at(stage, chunk)), rows)], peers[bit]
         else:
-            depth = [p[:2] for p in plans[which][0]].index(("reduce", bit))
             part, row = place_of(chunk)
-            src = grad_ref.at[part, pl.ds(aligned(row + kept(which, depth + 1)), rows)]
+            src = grad_ref.at[part, pl.ds(aligned(row + kept(bit + 3)), rows)]
             dst, target = src, peers[bit]
-        send = chunk if kind == "reduce" and not halving else which
+        send = chunk if kind == "reduce" and not halving else 0
         return pltpu.make_async_remote_copy(
             src_ref=src, dst_ref=dst, send_sem=r_sem.at[0, stage, send], recv_sem=r_sem.at[1, stage, chunk],
             device_id=target, device_id_type=MESH)
 
-    def land_at(which, stage, chunk):
-        at = 0
-        for kind, bit, rows, halving in plans[which][0][:stage]:
-            if kind == "reduce":
-                at += rows
-        size = sum(p[2] for p in plans[which][0] if p[0] == "reduce")
-        index = div(chunk, EVERY)
-        if which == 0:
-            index = index * (EVERY - 1) + mod(mod(chunk, EVERY) + EVERY - OFFSET - 1, EVERY)
-        return index * size + at
-
     def add(a, b):
         return (a.astype(F32) + b.astype(F32)).astype(BF)
 
-    def finish(which, stage, chunk):
-        copy_of(which, stage, chunk).wait_recv()
-        kind, bit, rows, halving = plans[which][1][stage]
-        both = ("side", 0) not in [p[:2] for p in plans[which][1][:stage]]
+    def finish(stage, chunk):
+        copy_of(stage, chunk).wait_recv()
+        kind, bit, rows, halving = plan[stage]
         base = chunk * CHUNK
-        last = stage == len(plans[which][0]) - 1
         if kind == "core":
             part, row = place_of(chunk)
             at = pl.ds(aligned(base), CHUNK)
             for n in (0, 1):
                 core_buf[n, at] = add(w[n, k, part, pl.ds(aligned(row), CHUNK)], core_buf[n, at])
         elif kind == "side":
-            at = pl.ds(aligned(base + kept(which, stage)), rows)
+            at = pl.ds(aligned(base), rows)
             side_buf[at] = add(core_buf[u, at], side_buf[at])
         elif kind == "reduce":
-            at = pl.ds(aligned(base + kept(which, stage + 1)), rows)
-            land = pl.ds(aligned(land_at(which, stage, chunk)), rows)
+            at = pl.ds(aligned(base + kept(stage + 1)), rows)
             if not halving:
-                copy_of(which, stage, chunk).wait_send()
-            if both:
-                for n in (0, 1):
-                    core_buf[n, at] = add(core_buf[n, at], lands[which][n, land])
-            elif last:
+                copy_of(stage, chunk).wait_send()
+            total = add(side_buf[at], land[pl.ds(aligned(land_at(stage, chunk)), rows)])
+            if stage == len(sums) - 1:
                 part, row = place_of(chunk)
-                grad_ref[part, pl.ds(aligned(row + kept(which, stage + 1)), rows)] = add(
-                    side_buf[at], lands[which][0, land])
+                grad_ref[part, pl.ds(aligned(row + kept(stage + 1)), rows)] = total
             else:
-                side_buf[at] = add(side_buf[at], lands[which][0, land])
-
-    starts = []
-    for which in (0, 1):
-        lags = list(LAGS[which]) + [1] * 32
-        starts.append([sum(lags[:n]) for n in range(len(plans[which][1]) + 1)])
-
-    def step(which, stage, chunk):
+                side_buf[at] = total
+
+    lags = list(LAGS) + [1] * 32
+    starts = [sum(lags[:n]) for n in range(n_all + 1)]
+
+    def step(stage, chunk):
         if stage > 0:
-            finish(which, stage - 1, chunk)
-        if stage < len(plans[which][1]):
-            copy_of(which, stage, chunk).start()
+            finish(stage - 1, chunk)
+        if stage < n_all:
+            copy_of(stage, chunk).start()
 
     def tick(i):
-        for which in (0, 1):
-            for stage in range(len(plans[which][1]) + 1):
-                chunk = i - starts[which][stage]
-                mine = lax.rem(chunk + EVERY, EVERY) == OFFSET
-                if which == 0:
-                    mine = jnp.logical_not(mine)
-
-                @pl.when((chunk >= 0) & (chunk < n_chunks) & mine)
-                def _():
-                    step(which, stage, chunk)
-
-    def ffn(i, _):
-        j, g = lax.div(i, N_TP), lax.rem(i, N_TP)
-        gu, gk = lax.div(g, 2), lax.rem(g, 2)
-        for at, work in ((0, lambda: step2(na + 1)), (1, lambda: step1(na + 2)), (2, lambda: step3(na + 1)),
-                         (3, lambda: step2(na + 2)), (4, lambda: step4(na + 1)), (6, lambda: step3(na + 2)),
-                         (8, lambda: step4(na + 2))):
-            @pl.when(i == at)
+        for stage in range(n_all + 1):
+            chunk = i - starts[stage]
+
+            @pl.when((chunk >= 0) & (chunk < n_chunks))
             def _():
-                work()
-
-        hid = pl.ds(pl.multiple_of(j * F_BLOCK, F_BLOCK), F_BLOCK)
-        up, down = w[gu, gk, 1, hid, :], w[gu, gk, 2, hid, :]
-        pre = dot(second[...], up, NT) + upb[g, :, hid]
+                step(stage, chunk)
+
+    def ffn(gu, start, size):
+        hid = pl.ds(pl.multiple_of(start, size), size)
+        up = w[gu, :, 1, hid, :].reshape(2 * size, features)
+        down = w[gu, :, 2, hid, :].reshape(2 * size, features)
+        pre = dot(second[...], up, NT) + jnp.concatenate([upb[2 * gu, :, hid], upb[2 * gu + 1, :, hid]], axis=1)
         act, slope = gelu_parts(pre)
         act = act.astype(BF)
         ff[...] += dot(act, down, NN)
         og = ogb[...].reshape(n_rows, features)
         pg = (dot(og, down, NT) * slope).astype(BF)
         sg[...] += dot(pg, up, NN)
-        w[gu, gk, 2, hid, :] = dot(act, og, TN).astype(BF)
-        w[gu, gk, 1, hid, :] = dot(pg, second[...], TN).astype(BF)
-        small[pl.ds(8 + g, 1), hid] = jnp.sum(pg.astype(F32), axis=0, keepdims=True)
-
-        @pl.when(i >= N_TP)
+        w[gu, :, 2, hid, :] = dot(act, og, TN).astype(BF).reshape(2, size, features)
+        w[gu, :, 1, hid, :] = dot(pg, second[...], TN).astype(BF).reshape(2, size, features)
+        sums = jnp.sum(pg.astype(F32), axis=0, keepdims=True)
+        for gk in (0, 1):
+            for m in range(size // 128):
+                at = gk * size + m * 128
+                upsum[(2 * gu + gk) * (hidden // 128) + lax.div(start, 128) + m] = sums[:, at : at + 128]
+
+    def hooks(i, *work):
+        for at, do in work:
+            @pl.when(i == at)
+            def _():
+                do()
+
+    def ffn_block(i, _):
+        hooks(i, (0, lambda: step2(na + 1)), (1, lambda: (step4(na), step1(na + 2))),
+              (2, lambda: (step_own(na + 1), step3(na + 1), step2(na + 2))),
+              (3, lambda: (step4(na + 1), step3(na + 2))), (4, lambda: step_own(na + 2)), (5, lambda: step4(na + 2)))
+        ffn(lax.rem(u + i, 2), lax.div(i, 2) * F_BLOCK, F_BLOCK)
+
+        @pl.when(i >= 2)
         def _():
-            tick(i - N_TP)
+            tick(2 * i - 4)
+            tick(2 * i - 3)
 
         return 0
 
-    lax.fori_loop(0, nf * N_TP, ffn, 0)
+    lax.fori_loop(0, nf * 2, ffn_block, 0)
     done = (nf - 1) * N_TP
+    for g in range(N_TP):
+        for m in range(hidden // 128):
+            small[8 + g : 9 + g, m * 128 : (m + 1) * 128] = upsum[g * (hidden // 128) + m]
 
     def middle_rows(i, _):
         b, here_rows, rows = rows_at(i)
@@ -519,23 +507,24 @@
 
     lax.fori_loop(0, n_rows // ROWS, middle_rows, 0)
 
-    def back_copy(n, i):
+    def back_copy(n, i, b):
         src, dst = ((outp, res_ref), (inp, ing_ref))[n]
         target = others[i]
-        return remote(src.at[:, pl.ds(target[1] * own_slots, own_slots)], dst.at[pl.ds(t * here, here)], o_sem,
-                      (n, i), target)
+        return remote(src.at[b, pl.ds(target[1] * own_slots, own_slots)], dst.at[t * here + b], b_sem, (n, i, b), target)
 
     def back_own(n):
         src, dst = ((outp, res_ref), (inp, ing_ref))[n]
         return pltpu.make_async_copy(src.at[:, pl.ds(t * own_slots, own_slots)], dst.at[pl.ds(t * here, here)],
                                      l_sem.at[n])
 
-    def send_back(n):
-        back_own(n).start()
-        for i in range(N_TP - 1):
-            back_copy(n, i).start()
-
-    send_back(0)
+    back_pieces = [(i, b) for i in range(N_TP - 1) for b in range(here)]
+
+    def send_back(n, at):
+        if at == 0:
+            back_own(n).start()
+        for i, b in back_pieces[at::4]:
+            back_copy(n, i, b).start()
+
     sg[...] = jnp.zeros_like(sg)
 
     def back_group(g, _):
@@ -576,7 +565,6 @@
         return 0
 
     lax.fori_loop(0, n_rows // ROWS, last_rows, 0)
-    send_back(1)
 
     small_targets = [core, side] + peers
 
@@ -585,32 +573,38 @@
 
     done = done + N_TP
 
+    def small_turn(n):
+        if n > len(small_targets):
+            return
+        if n > 0:
+            small_copy(n - 1).wait()
+            small[...] += small_buf[n - 1]
+        if n < len(small_targets):
+            small_copy(n).start()
+
     def rest_of(i, _):
         tick(i)
+        hooks(i, *((done + n, functools.partial(small_turn, n)) for n in range(n_chunks - done)))
         return 0
 
     lax.fori_loop(done, n_chunks, rest_of, 0)
     state = {}
     for chunk in range(n_chunks):
-        which = int(chunk % EVERY == OFFSET)
-        n_all = len(plans[which][1])
-        stage = max(n for n in range(n_all + 1) if chunk + starts[which][n] < n_chunks)
+        stage = max(n for n in range(n_all + 1) if chunk + starts[n] < n_chunks)
         if stage < n_all:
-            state[chunk] = (which, stage)
+            state[chunk] = stage
     turn = 0
     up_left = True
-    while state or turn <= len(small_targets):
-        if turn <= len(small_targets):
-            if turn > 0:
-                small_copy(turn - 1).wait()
-                small[...] += small_buf[turn - 1]
-            if turn < len(small_targets):
-                small_copy(turn).start()
+    small_left = list(range(n_chunks - done, len(small_targets) + 1))
+    while state or small_left:
+        for n, piece in BACK.get(("t", turn), ()):
+            send_back(n, piece)
+        if small_left:
+            small_turn(small_left.pop(0))
         for chunk in sorted(state):
-            which, stage = state[chunk]
-            step(which, stage + 1, chunk)
-            state[chunk] = (which, stage + 1)
-            if stage + 1 == len(plans[which][1]):
+            state[chunk] += 1
+            step(state[chunk], chunk)
+            if state[chunk] == n_all:
                 del state[chunk]
         if up_left and not [chunk for chunk in state if chunk < f_chunks]:
             up_left = False
@@ -624,24 +618,20 @@
     small_ref[7:8, :] = small[pl.ds(12 + t, 1), :]
 
     for n in (0, 1):
-        for i in range(N_TP - 1):
-            back_copy(n, i).wait_recv()
-            back_copy(n, i).wait_send()
+        for i, b in back_pieces:
+            back_copy(n, i, b).wait_recv()
+            back_copy(n, i, b).wait_send()
         back_own(n).wait()
     for n in range(5):
         for i in range(N_TP - 1):
             rows_copy(n, i).wait_send()
 
-    for which in (0, 1):
-        count = len([chunk for chunk in range(n_chunks) if (chunk % EVERY == OFFSET) == bool(which)])
-        for stage, (kind, _, rows, halving) in enumerate(plans[which][1]):
-            if kind != "reduce" or halving:
-                both = ("side", 0) not in [p[:2] for p in plans[which][1][:stage]]
-                view = core_buf.at[:, pl.ds(0, count * rows)] if both and kind != "side" else side_buf.at[
-                    pl.ds(0, count * rows)]
-                pltpu.make_async_remote_copy(
-                    src_ref=view, dst_ref=view, send_sem=r_sem.at[0, stage, which], recv_sem=r_sem.at[1, stage, which],
-                    device_id=core, device_id_type=MESH).wait_send()
+    for stage, (kind, _, rows, halving) in enumerate(plan):
+        if kind != "reduce" or halving:
+            view = core_buf if kind == "core" else side_buf.at[pl.ds(0, n_chunks * rows)]
+            pltpu.make_async_remote_copy(
+                src_ref=view, dst_ref=view, send_sem=r_sem.at[0, stage, 0], recv_sem=r_sem.at[1, stage, 0],
+                device_id=core, device_id_type=MESH).wait_send()
 
 
 def layer_call(n_clips, counts, tok, ext, og, proj, qkv, up, down, vectors, qv_bias, table):
@@ -655,9 +645,8 @@
     n_chunks = 3 * features // CHUNK
     heads = features // HD
     bits = n_clips.bit_length() - 1
-    sizes = [sum(p[2] for p in reduce_plan(n_clips, n)[0] if p[0] == "reduce") for n in (0, 1)]
-    n_all = max(len(reduce_plan(n_clips, n)[1]) for n in (0, 1))
-    n_second = -(-n_chunks // EVERY)
+    sums, plan = reduce_plan(n_clips)
+    n_all = len(plan)
     hbm = pl.BlockSpec(memory_space=pl.ANY)
     vmem = pl.BlockSpec(memory_space=pltpu.VMEM)
     smem = pl.BlockSpec(memory_space=pltpu.SMEM)
@@ -695,9 +684,9 @@
             pltpu.VMEM((here, slots, features), BF),
             pltpu.VMEM((2, 3 * features, features), BF),
             pltpu.VMEM((3 * features, features), BF),
-            pltpu.VMEM((1, n_second * (EVERY - 1) * sizes[0], features), BF),
-            pltpu.VMEM((2, n_second * sizes[1], features), BF),
+            pltpu.VMEM((n_chunks * sum(p[2] for p in sums[2:]), features), BF),
             pltpu.VMEM((16, features), F32),
+            pltpu.VMEM((N_TP * hidden // 128, 1, 128), F32),
             pltpu.VMEM((2 + bits, 16, features), F32),
             dma((3 + nf * features // F_BLOCK,)),
             dma((2, 5, N_TP - 1)),
@@ -708,6 +697,7 @@
             dma((2, n_all, n_chunks)),
             dma((2, 2 + bits)),
             dma((2, 3, N_TP - 1)),
+            dma((2, 2, N_TP - 1, here)),
         ],
         compiler_params=pltpu.CompilerParams(collective_id=0, has_side_effects=True, vmem_limit_bytes=VMEM_LIMIT),
         name="encoder_layer",

time: 188 us -> 179 us (0.952)
  Pallas kernels: 187 us -> 177 us
    pallas_call x1, Pallas kernels: 181 us -> 171 us  [layer_call(): pl.pallas_call(functools.partial(layer_kernel, (here, slots, width, hidde...]
where the time goes in v2:
time: 179 us; the launch traced here: 178 us
  Pallas kernels  177 us (99%)
    pallas_call x1, Pallas kernels, layer_call(): pl.pallas_call(functools.partial(layer_kernel, (here, slots, width, hidde...  171 us
    pallas_call x1, Pallas kernels, widen_call(): pl.pallas_call(widen_kernel, grid=(steps,), out_shape=(jax.ShapeDtypeStru...  6.9 us

profile of v2, /device:TPU:0, one launch (start us, length us, event | category | flops | bytes accessed | tf_op | source)
XLA Modules:
  0.0 178.2 jit_solution(635877964886695765)
XLA Ops:
  0.7 170.5 %encoder_layer.1 = (bf16[3,768,768]{2,1,0:T(8,128)(2,1)}, bf16[768,768]{1,0:T(8,128)(2,1)}, f32[8,768]{1,0:T(8,128)}, bf16[8,64,768]{2,1,0:T(8,128)(2,1)}, bf16[8,64,768]{2,1,0:T(8,128)(2,1)}) custom-call(s32[8]{0:T(128)} %count_ref.1, bf16[8,64,768]{2,1,0:T(8,128)(2,1)} %tok_ref.1, s32[8,64]{1,0:T(8,128)} %ext_ref.1, bf16[8,64,768]{2,1,0:T(8,128)(2,1)} %og_ref.1, ...), custom_call_target="tpu_custom_call" | custom-call | tf_op jit(solution)/shard_map/encoder_layer/pallas_call | solution.py:655
  171.2 6.9 %widen.1 = (f32[576,768]{1,0:T(8,128)}, f32[192,768]{1,0:T(8,128)}, f32[768,768]{1,0:T(8,128)}, f32[768,768]{1,0:T(8,128)}, f32[8,64,768]{2,1,0:T(8,128)}, /*ind...) custom-call(bf16[3,768,768]{2,1,0:T(8,128)(2,1)} %get-tuple-element., ...), custom_call_target="tpu_custom_call" | custom-call | tf_op jit(solution)/shard_map/widen/pallas_call | solution.py:738

commit v3 on v2

--- a/solution.py
+++ b/solution.py
@@ -79,7 +79,7 @@
     return (dx - m1 - xhat * m2) * rstd, jnp.sum(dy * xhat, axis=0, keepdims=True), jnp.sum(dy, axis=0, keepdims=True)
 
 
-LAGS = (1, 2, 2, 1, 1, 1, 1, 2)
+LAGS = (1, 2, 1, 1, 1, 1, 1, 2)
 BACK = {("t", 2): [(n, piece) for n in (0, 1) for piece in range(4)]}
 
 
@@ -249,7 +249,6 @@
     sg[...] = jnp.zeros_like(sg)
     step2(1)
     step2(2)
-    w_copy("y", na + 1).start()
     for n in (1, 3, 4, 0):
         wait_rows(n)
     start_rows(2)
@@ -330,8 +329,8 @@
                 probs[b, g * per_group + r] = p
                 mixed[g, r * HD : (r + 1) * HD, cols] = dot(value, p, NN).astype(BF)
 
-        for at, work in ((0, lambda: (step1(na), w_copy("y", na + 2).start())), (1, lambda: step1(na + 1)),
-                         (2, lambda: step2(na))):
+        for at, work in ((0, lambda: (step1(na), w_copy("y", na + 1).start())),
+                         (1, lambda: w_copy("y", na + 2).start()), (2, lambda: step2(na))):
             @pl.when(n == at)
             def _():
                 work()
@@ -471,20 +470,21 @@
                 do()
 
     def ffn_block(i, _):
-        hooks(i, (0, lambda: step2(na + 1)), (1, lambda: (step4(na), step1(na + 2))),
-              (2, lambda: (step_own(na + 1), step3(na + 1), step2(na + 2))),
-              (3, lambda: (step4(na + 1), step3(na + 2))), (4, lambda: step_own(na + 2)), (5, lambda: step4(na + 2)))
+        hooks(i, (0, lambda: step1(na + 1)), (1, lambda: step4(na)),
+              (2, lambda: (step_own(na + 1), step2(na + 1), step1(na + 2))),
+              (3, lambda: (step3(na + 1), step4(na + 1), step2(na + 2))),
+              (4, lambda: (step_own(na + 2), step3(na + 2))), (5, lambda: step4(na + 2)))
         ffn(lax.rem(u + i, 2), lax.div(i, 2) * F_BLOCK, F_BLOCK)
 
-        @pl.when(i >= 2)
+        @pl.when(i >= 1)
         def _():
-            tick(2 * i - 4)
-            tick(2 * i - 3)
+            tick(2 * i - 2)
+            tick(2 * i - 1)
 
         return 0
 
     lax.fori_loop(0, nf * 2, ffn_block, 0)
-    done = (nf - 1) * N_TP
+    done = 4 * nf - 2
     for g in range(N_TP):
         for m in range(hidden // 128):
             small[8 + g : 9 + g, m * 128 : (m + 1) * 128] = upsum[g * (hidden // 128) + m]
@@ -551,7 +551,10 @@
         sg[...] += dot(dqkv, w[gu, gk, 0, 0 : 3 * width, :], TN)
         w[gu, gk, 0, 0 : 3 * width, :] = dot(dqkv, first[...], NN).astype(BF)
         small[pl.ds(12 + g, 1), 0 : 3 * width] = dot(jnp.ones((8, n_rows), BF), dqkv, NT)[0:1]
-        tick(done + g)
+        @pl.when(lax.rem(g, 2) == 0)
+        def _():
+            tick(done + lax.div(g, 2))
+
         return 0
 
     lax.fori_loop(0, N_TP, back_group, 0)
@@ -571,7 +574,7 @@
     def small_copy(i):
         return remote(small, small_buf.at[i], s_sem, (i,), small_targets[i])
 
-    done = done + N_TP
+    done = done + N_TP // 2
 
     def small_turn(n):
         if n > len(small_targets):
@@ -601,7 +604,7 @@
             send_back(n, piece)
         if small_left:
             small_turn(small_left.pop(0))
-        for chunk in sorted(state):
+        for chunk in sorted(state, reverse=True):
             state[chunk] += 1
             step(state[chunk], chunk)
             if state[chunk] == n_all:
@@ -724,7 +727,7 @@
     _, features, _ = grads.shape
     hidden = up_grad.shape[1]
     count, own_slots, _ = rows_out.shape
-    steps = 4
+    steps = 2
     whole = pl.BlockSpec(memory_space=pltpu.VMEM)
 
     def rows_of(rows, first):

time: 179 us -> 170 us (0.950)
  Pallas kernels: 177 us -> 169 us
    pallas_call x1, Pallas kernels: 171 us -> 164 us  [layer_call(): pl.pallas_call(functools.partial(layer_kernel, (here, slots, width, hidde...]
where the time goes in v3:
time: 170 us
  Pallas kernels  169 us (99%)
    pallas_call x1, Pallas kernels, layer_call(): pl.pallas_call(functools.partial(layer_kernel, (here, slots, width, hidde...  164 us
    pallas_call x1, Pallas kernels, widen_call(): pl.pallas_call(widen_kernel, grid=(steps,), out_shape=(jax.ShapeDtypeStru...  5.92 us

profile of v3, /device:TPU:0, one launch (start us, length us, event | category | flops | bytes accessed | tf_op | source)
XLA Modules:
  0.0 170.3 jit_solution(6287797258042617073)
XLA Ops:
  0.7 163.6 %encoder_layer.1 = (bf16[3,768,768]{2,1,0:T(8,128)(2,1)}, bf16[768,768]{1,0:T(8,128)(2,1)}, f32[8,768]{1,0:T(8,128)}, bf16[8,64,768]{2,1,0:T(8,128)(2,1)}, bf16[8,64,768]{2,1,0:T(8,128)(2,1)}) custom-call(s32[8]{0:T(128)} %count_ref.1, bf16[8,64,768]{2,1,0:T(8,128)(2,1)} %tok_ref.1, s32[8,64]{1,0:T(8,128)} %ext_ref.1, bf16[8,64,768]{2,1,0:T(8,128)(2,1)} %og_ref.1, ...), custom_call_target="tpu_custom_call" | custom-call | tf_op jit(solution)/shard_map/encoder_layer/pallas_call | solution.py:658
  164.2 5.9 %widen.1 = (f32[576,768]{1,0:T(8,128)}, f32[192,768]{1,0:T(8,128)}, f32[768,768]{1,0:T(8,128)}, f32[768,768]{1,0:T(8,128)}, f32[8,64,768]{2,1,0:T(8,128)}, /*ind...) custom-call(bf16[3,768,768]{2,1,0:T(8,128)(2,1)} %get-tuple-element., ...), custom_call_target="tpu_custom_call" | custom-call | tf_op jit(solution)/shard_map/widen/pallas_call | solution.py:741

commit v4 on v3

--- a/solution.py
+++ b/solution.py
@@ -238,21 +238,6 @@
     for copy in row_copies():
         copy.wait()
 
-    step1(0)
-    start_rows(0)
-    small[...] = jnp.zeros_like(small)
-    step1(1)
-    step2(0)
-    step1(2)
-    w_copy("y", na).start()
-    ff[...] = jnp.zeros_like(ff)
-    sg[...] = jnp.zeros_like(sg)
-    step2(1)
-    step2(2)
-    for n in (1, 3, 4, 0):
-        wait_rows(n)
-    start_rows(2)
-
     per_clip = slots // ROWS
     sources = ROWS // own_slots
 
@@ -260,7 +245,7 @@
         return lax.div(i, per_clip), pl.ds(pl.multiple_of(lax.rem(i, per_clip) * ROWS, ROWS), ROWS), pl.ds(
             pl.multiple_of(i * ROWS, ROWS), ROWS)
 
-    def first_rows(i, _):
+    def place_rows(i, _):
         b, here_rows, rows = rows_at(i)
         line = lax.broadcasted_iota(jnp.int32, (2 * TABLE, own_slots), 0) & (TABLE - 1)
         pos = []
@@ -272,12 +257,33 @@
             lo = dot(hot[1], table_ref[2 * TABLE :, :], TN)
             sh, ch, sl, cl = hi[:, :half], hi[:, half:], lo[:, :half], lo[:, half:]
             pos.append(jnp.concatenate([sh * cl + ch * sl, ch * cl - sh * sl], axis=1))
-        v = tokb[b, here_rows, :].astype(F32) + jnp.concatenate(pos, axis=0)
+        stream[rows, :] = jnp.concatenate(pos, axis=0)
+        return 0
+
+    def first_rows(i, _):
+        b, here_rows, rows = rows_at(i)
+        v = tokb[b, here_rows, :].astype(F32) + stream[rows, :]
         stream[rows, :] = v
         xhat, _ = stats(v)
         first[rows, :] = (xhat * row(gain1_ref) + row(bias1_ref)).astype(BF)
         return 0
 
+    step1(0)
+    small[...] = jnp.zeros_like(small)
+    step1(1)
+    start_rows(0)
+    step2(0)
+    step1(2)
+    ff[...] = jnp.zeros_like(ff)
+    sg[...] = jnp.zeros_like(sg)
+    step2(1)
+    step2(2)
+    w_copy("y", na).start()
+    for n in (1, 3, 4):
+        wait_rows(n)
+    lax.fori_loop(0, n_rows // ROWS, place_rows, 0)
+    wait_rows(0)
+    start_rows(2)
     lax.fori_loop(0, n_rows // ROWS, first_rows, 0)
     for i in range(na):
         step_own(i)
@@ -567,7 +573,6 @@
         small[1:2, :] += dbias
         return 0
 
-    lax.fori_loop(0, n_rows // ROWS, last_rows, 0)
 
     small_targets = [core, side] + peers
 
@@ -587,6 +592,7 @@
 
     def rest_of(i, _):
         tick(i)
+        hooks(i, (done, lambda: lax.fori_loop(0, n_rows // ROWS, last_rows, 0)))
         hooks(i, *((done + n, functools.partial(small_turn, n)) for n in range(n_chunks - done)))
         return 0
 

time: 170 us -> 168 us (0.988)
  Pallas kernels: 169 us -> 167 us
    pallas_call x1, Pallas kernels: 164 us -> 161 us  [layer_call(): pl.pallas_call(functools.partial(layer_kernel, (here, slots, width, hidde...]
where the time goes in v4:
time: 168 us
  Pallas kernels  167 us (99%)
    pallas_call x1, Pallas kernels, layer_call(): pl.pallas_call(functools.partial(layer_kernel, (here, slots, width, hidde...  161 us
    pallas_call x1, Pallas kernels, widen_call(): pl.pallas_call(widen_kernel, grid=(steps,), out_shape=(jax.ShapeDtypeStru...  5.92 us

profile of v4, /device:TPU:0, one launch (start us, length us, event | category | flops | bytes accessed | tf_op | source)
XLA Modules:
  0.0 167.9 jit_solution(16244430478703383669)
XLA Ops:
  0.7 161.1 %encoder_layer.1 = (bf16[3,768,768]{2,1,0:T(8,128)(2,1)}, bf16[768,768]{1,0:T(8,128)(2,1)}, f32[8,768]{1,0:T(8,128)}, bf16[8,64,768]{2,1,0:T(8,128)(2,1)}, bf16[8,64,768]{2,1,0:T(8,128)(2,1)}) custom-call(s32[8]{0:T(128)} %count_ref.1, bf16[8,64,768]{2,1,0:T(8,128)(2,1)} %tok_ref.1, s32[8,64]{1,0:T(8,128)} %ext_ref.1, bf16[8,64,768]{2,1,0:T(8,128)(2,1)} %og_ref.1, ...), custom_call_target="tpu_custom_call" | custom-call | tf_op jit(solution)/shard_map/encoder_layer/pallas_call | solution.py:664
  161.8 5.9 %widen.1 = (f32[576,768]{1,0:T(8,128)}, f32[192,768]{1,0:T(8,128)}, f32[768,768]{1,0:T(8,128)}, f32[768,768]{1,0:T(8,128)}, f32[8,64,768]{2,1,0:T(8,128)}, /*ind...) custom-call(bf16[3,768,768]{2,1,0:T(8,128)(2,1)} %get-tuple-element., ...), custom_call_target="tpu_custom_call" | custom-call | tf_op jit(solution)/shard_map/widen/pallas_call | solution.py:747

commit v5 on v4

--- a/solution.py
+++ b/solution.py
@@ -98,9 +98,9 @@
 
 def layer_kernel(dims, n_clips, count_ref, tok_ref, ext_ref, og_ref, proj_ref, qkv_ref, up_ref, down_ref,
                  gain1_ref, bias1_ref, gain2_ref, bias2_ref, projb_ref, downb_ref, upb_ref, qvb_ref, table_ref,
-                 grad_ref, upg_ref, small_ref, res_ref, ing_ref,
+                 grad_out, up_out, small_ref, res_ref, ing_ref,
                  w, tokb, extb, ogb, qvb, upb, stream, first, qkvt, probs, mixed, middle, second, ff, sg, branch, outp,
-                 inp, core_buf, side_buf, land, small, upsum, small_buf, l_sem, t_sem, y_sem, q_sem, f_sem, c_sem,
+                 inp, core_buf, side_buf, land, grad_ref, upg_ref, small, upsum, small_buf, l_sem, t_sem, y_sem, q_sem, f_sem, c_sem,
                  r_sem, s_sem, o_sem, b_sem):
     here, slots, width, hidden, features = dims
     bits = n_clips.bit_length() - 1
@@ -604,6 +604,9 @@
             state[chunk] = stage
     turn = 0
     up_left = True
+    out_copies = [pltpu.make_async_copy(grad_ref.at[2], grad_out.at[2], l_sem.at[2]),
+                  pltpu.make_async_copy(upg_ref, up_out, l_sem.at[3]),
+                  pltpu.make_async_copy(grad_ref.at[0], grad_out.at[0], l_sem.at[4])]
     small_left = list(range(n_chunks - done, len(small_targets) + 1))
     while state or small_left:
         for n, piece in BACK.get(("t", turn), ()):
@@ -621,7 +624,10 @@
                 for j in range(nf):
                     upg_ref[m * F_BLOCK : (m + 1) * F_BLOCK, j * F_BLOCK : (j + 1) * F_BLOCK] = grad_ref[
                         1, j * F_BLOCK : (j + 1) * F_BLOCK, m * F_BLOCK : (m + 1) * F_BLOCK].T
+            out_copies[0].start()
+            out_copies[1].start()
         turn += 1
+    out_copies[2].start()
     small_ref[0:6, :] = small[0:6, :]
     small_ref[6:7, :] = small[pl.ds(8 + t, 1), :]
     small_ref[7:8, :] = small[pl.ds(12 + t, 1), :]
@@ -635,6 +641,8 @@
         for i in range(N_TP - 1):
             rows_copy(n, i).wait_send()
 
+    for copy in out_copies:
+        copy.wait()
     for stage, (kind, _, rows, halving) in enumerate(plan):
         if kind != "reduce" or halving:
             view = core_buf if kind == "core" else side_buf.at[pl.ds(0, n_chunks * rows)]
@@ -671,7 +679,7 @@
             jax.ShapeDtypeStruct((count, own_slots, features), BF),
         ),
         in_specs=[smem, hbm, vmem] + [hbm] * 5 + [vmem] * 9,
-        out_specs=(vmem, vmem, vmem, hbm, hbm),
+        out_specs=(hbm, hbm, vmem, hbm, hbm),
         scratch_shapes=[
             pltpu.VMEM((2, 2, 3, features, features), BF),
             pltpu.VMEM((here, slots, features), BF),
@@ -694,6 +702,8 @@
             pltpu.VMEM((2, 3 * features, features), BF),
             pltpu.VMEM((3 * features, features), BF),
             pltpu.VMEM((n_chunks * sum(p[2] for p in sums[2:]), features), BF),
+            pltpu.VMEM((3, features, features), BF),
+            pltpu.VMEM((features, hidden), BF),
             pltpu.VMEM((16, features), F32),
             pltpu.VMEM((N_TP * hidden // 128, 1, 128), F32),
             pltpu.VMEM((2 + bits, 16, features), F32),

time: 168 us -> 167 us (level)
  no operation moved by 1% of the time
where the time goes in v5:
time: 167 us
  Pallas kernels  166 us (99%)
    pallas_call x1, Pallas kernels, layer_call(): pl.pallas_call(functools.partial(layer_kernel, (here, slots, width, hidde...  160 us
    pallas_call x1, Pallas kernels, widen_call(): pl.pallas_call(widen_kernel, grid=(steps,), out_shape=(jax.ShapeDtypeStru...  5.92 us

profile of v5, /device:TPU:0, one launch (start us, length us, event | category | flops | bytes accessed | tf_op | source)
XLA Modules:
  0.0 166.9 jit_solution(12687741534610428432)
XLA Ops:
  0.7 160.2 %encoder_layer.1 = (bf16[3,768,768]{2,1,0:T(8,128)(2,1)}, bf16[768,768]{1,0:T(8,128)(2,1)}, f32[8,768]{1,0:T(8,128)}, bf16[8,64,768]{2,1,0:T(8,128)(2,1)}, bf16[8,64,768]{2,1,0:T(8,128)(2,1)}) custom-call(s32[8]{0:T(128)} %count_ref.1, bf16[8,64,768]{2,1,0:T(8,128)(2,1)} %tok_ref.1, s32[8,64]{1,0:T(8,128)} %ext_ref.1, bf16[8,64,768]{2,1,0:T(8,128)(2,1)} %og_ref.1, ...), custom_call_target="tpu_custom_call" | custom-call | tf_op jit(solution)/shard_map/encoder_layer/pallas_call | solution.py:672
  160.8 5.9 %widen.1 = (f32[576,768]{1,0:T(8,128)}, f32[192,768]{1,0:T(8,128)}, f32[768,768]{1,0:T(8,128)}, f32[768,768]{1,0:T(8,128)}, f32[8,64,768]{2,1,0:T(8,128)}, /*ind...) custom-call(bf16[3,768,768]{2,1,0:T(8,128)(2,1)} %get-tuple-element., ...), custom_call_target="tpu_custom_call" | custom-call | tf_op jit(solution)/shard_map/widen/pallas_call | solution.py:757
